TPU v7x, 32 devices: a whole 2x2x4 slice. The times are simulated.
32 devices in a mesh: ex: 16 (over z, y, x), tp: 2 (over core).
Axes of the slice: x: 2, y: 2, z: 4, core: 2. Of those that a mesh axis runs over, the one named last changes fastest.
Arguments:
- tokens: bfloat16 [8192, 1024], P('ex'), may hold values from -6 to 6
- cotangent: bfloat16 [8192, 1024], P('ex'), may hold values from -6 to 6
- gain_one: float32 [1024], replicated, may hold values from 0.5 to 1.5
- w_query: bfloat16 [1024, 1024], P(None, 'tp'), may hold values from -0.1875 to 0.1875
- key_weight: bfloat16 [1024, 512], P(None, 'tp'), may hold values from -0.1875 to 0.1875
- value_weight: bfloat16 [1024, 512], P(None, 'tp'), may hold values from -0.1875 to 0.1875
- w_out: bfloat16 [1024, 1024], P('tp'), may hold values from -1.5 to 1.5
- gain_two: float32 [1024], replicated, may hold values from 0.5 to 1.5
- router: float32 [1024, 16], replicated, may hold values from -0.09375 to 0.09375
- w_gate: bfloat16 [16, 1024, 512], P('ex', None, 'tp'), may hold values from -0.1875 to 0.1875
- w_up: bfloat16 [16, 1024, 512], P('ex', None, 'tp'), may hold values from -0.1875 to 0.1875
- w_down: bfloat16 [16, 512, 1024], P('ex', 'tp'), may hold values from -1.5 to 1.5
- expert_ids: int32 [8192, 8], P('ex'), may hold values from 0 to 15, all different within a row; in each aligned block of 512 rows (0 to 511, 512 to 1023, ...) at most 512 rows name the same one
- leading_sequence_length: int32 [16], P('ex'), may hold values from 128 to 512, as said below
Outputs:
- output: bfloat16 [8192, 1024], P('ex')
- grad_tokens: bfloat16 [8192, 1024], P('ex')
- grad_gain_one: float32 [1024], replicated
- grad_query: float32 [1024, 1024], P(None, 'tp')
- grad_key: float32 [1024, 512], P(None, 'tp')
- grad_value: float32 [1024, 512], P(None, 'tp')
- grad_out_proj: float32 [1024, 1024], P('tp')
- grad_gain_two: float32 [1024], replicated
- grad_router: float32 [1024, 16], replicated
- grad_gate: float32 [16, 1024, 512], P('ex', None, 'tp')
- grad_up: float32 [16, 1024, 512], P('ex', None, 'tp')
- grad_down: float32 [16, 512, 1024], P('ex', 'tp')
Inputs may be any that keep to these rules, and one draw needn't show every extreme that they name: `expert_ids`: among the 512 rows of one block of tokens, each row names 8 different experts and no expert is named by more than 512 rows. `leading_sequence_length`: the second sequence of a block holds the remaining tokens and may be empty.
All inputs are finite; a program needn't handle non-finite values.
Results may differ from a plain program's by a relative error of at most 0.024.
Values may be sent and summed in bfloat16 or wider, within the bound.
No kernel may reach another device: no remote copies, remote signals or barrier semaphores. Data moves between devices by JAX's collectives and lax.ppermute only.
A program may use at most 256 MiB of HBM per device.

v0:
```python
import jax
import jax.numpy as jnp
from jax import lax
from jax.sharding import PartitionSpec as P

QUERY_HEADS = 16
KEY_VALUE_HEADS = 8
HEAD_SIZE = 64


EPS = 1e-06
THETA = 10000.0
NEGATIVE = -1e30
HIGH = lax.Precision.HIGHEST


def norm_scale(value_rows):
    return lax.rsqrt(jnp.mean(value_rows * value_rows, axis=-1, keepdims=True) + EPS)


def norm_backward(value_rows, scale, gain, grad):
    weighted = grad * gain
    inner = jnp.mean(weighted * value_rows, axis=-1, keepdims=True)
    grad_input = scale * weighted - value_rows * scale * scale * scale * inner
    grad_gain = jnp.sum(grad * value_rows * scale, axis=0)
    return (grad_input, grad_gain)


def rope_tables(length, split, width):
    index = jnp.arange(length, dtype=jnp.int32)
    second = index >= split
    place = jnp.where(second, index - split, index).astype(jnp.float32)
    freq = THETA ** (-(jnp.arange(width // 2, dtype=jnp.float32) * 2.0 / width))
    angle = place[:, None] * freq[None, :]
    return (jnp.cos(angle)[:, None, None, :], jnp.sin(angle)[:, None, None, :], second)


def apply_rotary(value_rows, cosine_table, sine_table):
    middle = value_rows.shape[-1] // 2
    front = value_rows[..., :middle]
    back = value_rows[..., middle:]
    return jnp.concatenate(
        [front * cosine_table - back * sine_table, back * cosine_table + front * sine_table],
        axis=-1,
    )


def rotate_back(grad, cosine_table, sine_table):
    middle = grad.shape[-1] // 2
    front = grad[..., :middle]
    back = grad[..., middle:]
    return jnp.concatenate(
        [front * cosine_table + back * sine_table, back * cosine_table - front * sine_table],
        axis=-1,
    )


def block_scores(query_block, key_rows, offset, second, factor):
    raw = jnp.einsum("qkgd,skd->kgqs", query_block, key_rows, preferred_element_type=jnp.float32)
    height = query_block.shape[0]
    row_index = offset + jnp.arange(height, dtype=jnp.int32)
    col_index = jnp.arange(key_rows.shape[0], dtype=jnp.int32)
    allowed = (col_index[None, :] <= row_index[:, None]) & (second[None, :] == second[:, None])
    return jnp.where(allowed, raw * factor, NEGATIVE)


def shards(
    tokens,
    cotangent,
    gain_one,
    w_query,
    key_weight,
    value_weight,
    w_out,
    gain_two,
    router,
    w_gate,
    w_up,
    w_down,
    expert_ids,
    leading_sequence_length,
):
    length = tokens.shape[0]
    width = tokens.shape[1]
    topk = expert_ids.shape[1]
    experts = lax.axis_size("ex")
    capacity = min(length, 2 * length * topk // experts)
    share = capacity // lax.axis_size("tp")
    query_group = QUERY_HEADS // KEY_VALUE_HEADS
    kv_local = key_weight.shape[1] // HEAD_SIZE
    q_width = w_query.shape[1]
    block = min(512, length)
    factor = float(HEAD_SIZE) ** (-0.5)
    x_full = tokens.astype(jnp.float32)
    scale_one = norm_scale(x_full)
    normed_one = (x_full * scale_one * gain_one).astype(jnp.bfloat16)
    cosine_table, sine_table, second = rope_tables(length, leading_sequence_length[0], HEAD_SIZE)
    query_pre = jnp.dot(normed_one, w_query, preferred_element_type=jnp.float32).reshape(
        length, kv_local, query_group, HEAD_SIZE
    )
    query_rows = apply_rotary(query_pre, cosine_table, sine_table).astype(jnp.bfloat16)
    key_pre = jnp.dot(normed_one, key_weight, preferred_element_type=jnp.float32).reshape(
        length, kv_local, 1, HEAD_SIZE
    )
    key_rows = apply_rotary(key_pre, cosine_table, sine_table).astype(jnp.bfloat16)[:, :, 0, :]
    value_rows = (
        jnp.dot(normed_one, value_weight, preferred_element_type=jnp.float32)
        .astype(jnp.bfloat16)
        .reshape(length, kv_local, HEAD_SIZE)
    )

    def forward_block(offset):
        scores = block_scores(query_rows, key_rows, offset, second, factor)
        largest = jnp.max(scores, axis=-1, keepdims=True)
        weights = jnp.exp(scores - largest)
        total = jnp.sum(weights, axis=-1, keepdims=True)
        probs = (weights / total).astype(jnp.bfloat16)
        result = jnp.einsum("kgqs,skd->qkgd", probs, value_rows, preferred_element_type=jnp.float32)
        return (result.astype(jnp.bfloat16), (largest + jnp.log(total))[..., 0])

    offsets = jnp.arange(length // block, dtype=jnp.int32) * block
    head_blocks, log_totals = lax.map(forward_block, offsets)
    heads = head_blocks.reshape(length, q_width)
    attention_output = lax.psum(jnp.dot(heads, w_out, preferred_element_type=jnp.float32), "tp")
    mixed = x_full + attention_output
    scale_two = norm_scale(mixed)
    normed_two = mixed * scale_two * gain_two
    routed = normed_two.astype(jnp.bfloat16)
    logits = jnp.dot(normed_two, router, precision=HIGH)
    expert_iota = jnp.arange(router.shape[1], dtype=jnp.int32)
    matches = expert_ids[:, :, None] == expert_iota[None, None, :]
    chosen = jnp.sum(jnp.where(matches, logits[:, None, :], 0.0), axis=-1)
    gates = jax.nn.softmax(chosen, axis=-1)
    pair_total = length * topk
    flat_ids = expert_ids.reshape(pair_total)
    hits = (flat_ids[:, None] == expert_iota[None, :]).astype(jnp.int32)
    rank = jnp.sum(jnp.cumsum(hits, axis=0) * hits, axis=1) - 1
    table = (
        jnp.full((capacity, experts), pair_total, jnp.int32)
        .at[rank, flat_ids]
        .set(jnp.arange(pair_total, dtype=jnp.int32))
    )
    tp_place = lax.axis_index("tp")
    padded = jnp.concatenate([routed, jnp.zeros((1, width), jnp.bfloat16)], axis=0)
    received = lax.all_to_all(padded[table // topk], "ex", split_axis=1, concat_axis=1, tiled=True)
    gate_w = w_gate[0]
    up_w = w_up[0]
    down_w = w_down[0]
    pre_gate = jnp.einsum("cnd,df->cnf", received, gate_w, preferred_element_type=jnp.float32)
    pre_up = jnp.einsum("cnd,df->cnf", received, up_w, preferred_element_type=jnp.float32)
    hidden = (jax.nn.silu(pre_gate) * pre_up).astype(jnp.bfloat16)
    expert_sum = lax.psum_scatter(
        jnp.einsum("cnf,fd->cnd", hidden, down_w, preferred_element_type=jnp.float32).astype(
            jnp.bfloat16
        ),
        "tp",
        scatter_dimension=0,
        tiled=True,
    )
    returned = lax.all_to_all(expert_sum, "ex", split_axis=1, concat_axis=1, tiled=True)
    grad_out = cotangent.astype(jnp.float32)
    local_rank = rank - tp_place * share
    inside = ((local_rank >= 0) & (local_rank < share)).reshape(length, topk)
    flat_place = (jnp.where(local_rank >= 0, local_rank, 0) * experts + flat_ids).reshape(
        length, topk
    )
    flat_place = jnp.where(inside, flat_place, 0)
    flat_returned = returned.reshape(share * experts, width)
    mixture = jnp.zeros((length, width), jnp.float32)
    gate_parts = []
    for choice_index in range(topk):
        picked = flat_returned[flat_place[:, choice_index]].astype(jnp.float32)
        picked = jnp.where(inside[:, choice_index : choice_index + 1], picked, 0.0)
        mixture = mixture + gates[:, choice_index : choice_index + 1] * picked
        gate_parts.append(jnp.sum(picked * grad_out, axis=1))
    mixture, gate_grads = (
        lax.psum(mixture.astype(jnp.bfloat16), "tp").astype(jnp.float32),
        lax.psum(jnp.stack(gate_parts, axis=1).astype(jnp.bfloat16), "tp").astype(jnp.float32),
    )
    output = (mixed + mixture).astype(jnp.bfloat16)
    grad_chosen = gates * (gate_grads - jnp.sum(gates * gate_grads, axis=1, keepdims=True))
    grad_logits = jnp.sum(jnp.where(matches, grad_chosen[:, :, None], 0.0), axis=1)
    grad_router = jnp.dot(normed_two.T, grad_logits, precision=HIGH)
    grad_normed_two = jnp.dot(grad_logits, router.T, precision=HIGH)
    grad_padded = jnp.concatenate([grad_out, jnp.zeros((1, width), jnp.float32)], axis=0)
    gate_padded = jnp.concatenate([gates.reshape(pair_total), jnp.zeros((1,), jnp.float32)], axis=0)
    grad_send = (grad_padded[table // topk] * gate_padded[table][:, :, None]).astype(jnp.bfloat16)
    grad_rows = lax.all_to_all(grad_send, "ex", split_axis=1, concat_axis=1, tiled=True)
    grad_hidden = jnp.einsum("cnd,fd->cnf", grad_rows, down_w, preferred_element_type=jnp.float32)
    sigmoid = jax.nn.sigmoid(pre_gate)
    activated = pre_gate * sigmoid
    grad_pre_gate = (grad_hidden * pre_up * sigmoid * (1.0 + pre_gate * (1.0 - sigmoid))).astype(
        jnp.bfloat16
    )
    grad_pre_up = (grad_hidden * activated).astype(jnp.bfloat16)
    grad_down = jnp.einsum("cnf,cnd->fd", hidden, grad_rows, preferred_element_type=jnp.float32)
    grad_gate = jnp.einsum(
        "cnd,cnf->df", received, grad_pre_gate, preferred_element_type=jnp.float32
    )
    grad_up = jnp.einsum("cnd,cnf->df", received, grad_pre_up, preferred_element_type=jnp.float32)
    gate_term = jnp.einsum("cnf,df->cnd", grad_pre_gate, gate_w, preferred_element_type=jnp.float32)
    input_sum = lax.psum_scatter(
        (
            gate_term
            + jnp.einsum("cnf,df->cnd", grad_pre_up, up_w, preferred_element_type=jnp.float32)
        ).astype(jnp.bfloat16),
        "tp",
        scatter_dimension=0,
        tiled=True,
    )
    input_returned = lax.all_to_all(input_sum, "ex", split_axis=1, concat_axis=1, tiled=True)
    flat_input = input_returned.reshape(share * experts, width)
    grad_moe = jnp.zeros((length, width), jnp.float32)
    for choice_index in range(topk):
        picked = flat_input[flat_place[:, choice_index]].astype(jnp.float32)
        grad_moe = grad_moe + jnp.where(inside[:, choice_index : choice_index + 1], picked, 0.0)
    grad_moe = lax.psum(grad_moe.astype(jnp.bfloat16), "tp").astype(jnp.float32)
    grad_normed_two = grad_normed_two + grad_moe
    grad_mixed_norm, grad_gain_two = norm_backward(mixed, scale_two, gain_two, grad_normed_two)
    grad_mixed = grad_out + grad_mixed_norm
    grad_attended = grad_mixed.astype(jnp.bfloat16)
    grad_out_proj = jnp.einsum(
        "th,td->hd", heads, grad_attended, preferred_element_type=jnp.float32
    )
    grad_heads = jnp.einsum("td,hd->th", grad_attended, w_out, preferred_element_type=jnp.float32)
    grad_heads = grad_heads.astype(jnp.bfloat16).reshape(length, kv_local, query_group, HEAD_SIZE)

    def backward_block(carry, pieces):
        offset, block_totals = pieces
        grad_keys, grad_values = carry
        scores = block_scores(query_rows, key_rows, offset, second, factor)
        probs = jnp.exp(scores - block_totals[..., None])
        probs_low = probs.astype(jnp.bfloat16)
        grad_probs = jnp.einsum(
            "qkgd,skd->kgqs", grad_heads, value_rows, preferred_element_type=jnp.float32
        )
        inner = jnp.sum(probs * grad_probs, axis=-1, keepdims=True)
        grad_scores = (probs * (grad_probs - inner) * factor).astype(jnp.bfloat16)
        grad_query_block = jnp.einsum(
            "kgqs,skd->qkgd", grad_scores, key_rows, preferred_element_type=jnp.float32
        )
        grad_keys = grad_keys + jnp.einsum(
            "kgqs,qkgd->skd", grad_scores, query_rows, preferred_element_type=jnp.float32
        )
        grad_values = grad_values + jnp.einsum(
            "kgqs,qkgd->skd", probs_low, grad_heads, preferred_element_type=jnp.float32
        )
        return ((grad_keys, grad_values), grad_query_block)

    empty = jnp.zeros((length, kv_local, HEAD_SIZE), jnp.float32)
    (grad_keys, grad_values), grad_query_blocks = lax.scan(
        backward_block, (empty, empty), (offsets, log_totals)
    )
    grad_queries = rotate_back(
        grad_query_blocks.reshape(length, kv_local, query_group, HEAD_SIZE),
        cosine_table,
        sine_table,
    )
    grad_queries = grad_queries.astype(jnp.bfloat16).reshape(length, q_width)
    grad_keys_pre = (
        rotate_back(grad_keys[:, :, None, :], cosine_table, sine_table)
        .astype(jnp.bfloat16)
        .reshape(length, kv_local * HEAD_SIZE)
    )
    grad_values_low = grad_values.astype(jnp.bfloat16).reshape(length, kv_local * HEAD_SIZE)
    grad_query = jnp.einsum(
        "td,th->dh", normed_one, grad_queries, preferred_element_type=jnp.float32
    )
    grad_key = jnp.einsum(
        "td,th->dh", normed_one, grad_keys_pre, preferred_element_type=jnp.float32
    )
    grad_value = jnp.einsum(
        "td,th->dh", normed_one, grad_values_low, preferred_element_type=jnp.float32
    )
    grad_normed_one = jnp.einsum(
        "th,dh->td", grad_queries, w_query, preferred_element_type=jnp.float32
    )
    grad_normed_one = grad_normed_one + jnp.einsum(
        "th,dh->td", grad_keys_pre, key_weight, preferred_element_type=jnp.float32
    )
    grad_normed_one = grad_normed_one + jnp.einsum(
        "th,dh->td", grad_values_low, value_weight, preferred_element_type=jnp.float32
    )
    grad_normed_one = lax.psum(grad_normed_one.astype(jnp.bfloat16), "tp").astype(jnp.float32)
    grad_input_norm, grad_gain_one = norm_backward(x_full, scale_one, gain_one, grad_normed_one)
    grad_tokens = (grad_mixed + grad_input_norm).astype(jnp.bfloat16)
    summed = (
        lax.psum(grad_query.astype(jnp.bfloat16), "ex").astype(jnp.float32),
        lax.psum(grad_key.astype(jnp.bfloat16), "ex").astype(jnp.float32),
        lax.psum(grad_value.astype(jnp.bfloat16), "ex").astype(jnp.float32),
        lax.psum(grad_out_proj.astype(jnp.bfloat16), "ex").astype(jnp.float32),
        lax.psum(grad_gain_one.astype(jnp.bfloat16), "ex").astype(jnp.float32),
        lax.psum(grad_gain_two.astype(jnp.bfloat16), "ex").astype(jnp.float32),
        lax.psum(grad_router.astype(jnp.bfloat16), "ex").astype(jnp.float32),
    )
    return (
        output,
        grad_tokens,
        summed[4],
        summed[0],
        summed[1],
        summed[2],
        summed[3],
        summed[5],
        summed[6],
        grad_gate[None],
        grad_up[None],
        grad_down[None],
    )


def solution(mesh):
    placed = (
        P("ex", None),
        P("ex", None),
        P(),
        P(None, "tp"),
        P(None, "tp"),
        P(None, "tp"),
        P("tp", None),
        P(),
        P(),
        P("ex", None, "tp"),
        P("ex", None, "tp"),
        P("ex", "tp", None),
        P("ex", None),
        P("ex"),
    )
    return jax.shard_map(
        shards,
        mesh=mesh,
        in_specs=placed,
        out_specs=(
            P("ex", None),
            P("ex", None),
            P(),
            P(None, "tp"),
            P(None, "tp"),
            P(None, "tp"),
            P("tp", None),
            P(),
            P(),
            P("ex", None, "tp"),
            P("ex", None, "tp"),
            P("ex", "tp", None),
        ),
        check_vma=False,
    )
```

profile of v0, /device:TPU:0, one launch (start us, length us, event | category | flops | bytes accessed | tf_op | source)
XLA Modules:
  0.0 1886.2 jit_solution(4936397912683765164)
XLA Ops:
  30.4 15.8 scatter_custom_fusion
  51.4 35.5 %gather_fusion = bf16[8192,1024]{1,0:T(8,128)(2,1)} fusion(bf16[513,1024]{1,0:T(8,128)(2,1)S(1)} %concatenate.41, s32[8192]{0:T(1024)S(1)} %broadcast_clamp_fusion.1), kind=kCustom, calls=%fused_computation | custom fusion | bytes 33587200 | tf_op jit(solution)/shard_map/gather | solution.py:145
  86.8 15.4 copy.106
  102.2 370.6 %all_to_all.20 = bf16[512,16,1024]{2,0,1:T(8,128)(2,1)S(1)} all-to-all(bf16[512,16,1024]{2,0,1:T(8,128)(2,1)S(1)} %copy.106), channel_id=1, replica_groups=mesh['ex'=16,'tp'=2] {'ex'}, dimensions={1} | all-to-all | bytes 33554432 | tf_op jit(solution)/shard_map/all_to_all | solution.py:145
  472.8 5.7 copy-done.1
  478.5 6.7 fusion.62
  485.3 18.1 multiply_convert_fusion.2
  503.3 10.4 convolution_convert_fusion
  513.8 24.7 %reduce-scatter.3.cloned.1.call-done = bf16[256,16,1024]{2,0,1:T(8,128)(2,1)} async-done(((bf16[512,16,1024]{2,0,1:T(8,128)(2,1)}), bf16[256,16,1024]{2,0,1:T(8,128)(2,1)}) %reduce-scatter.3.cloned.1.call-update) | async-done | bytes 8388624 | tf_op jit(solution)/shard_map/reduce_scatter | solution.py:152
  538.5 6.9 all-to-all-start.1
  547.5 44.6 %gather_fusion.9 = f32[8192,1024]{1,0:T(8,128)} fusion(f32[513,1024]{1,0:T(8,128)S(1)} %concatenate.43, s32[8192]{0:T(1024)S(1)} %broadcast_clamp_fusion.1), kind=kCustom, calls=%fused_computation.9 | custom fusion | bytes 67141632 | tf_op jit(solution)/shard_map/gather | solution.py:187
  596.3 108.1 %all-to-all-done.1 = bf16[256,16,1024]{2,0,1:T(8,128)(2,1)} async-done(((bf16[256,16,1024]{2,0,1:T(8,128)(2,1)}), bf16[256,16,1024]{2,0,1:T(8,128)(2,1)}, u32[]{:S(2)}, u32[]{:S(2)}) %all-to-all-start.1) | async-done | bytes 8388640 | tf_op jit(solution)/shard_map/all_to_all | solution.py:160
  704.5 11.3 copy.107
  715.8 7.2 gather_fusion.8
  723.0 7.8 gather_fusion.7
  730.8 8.3 gather_fusion.6
  739.1 7.9 gather_fusion.5
  747.0 7.9 gather_fusion.4
  755.0 7.9 gather_fusion.3
  762.9 8.3 gather_fusion.2
  771.2 7.9 gather_fusion.1
  788.7 45.5 %gather_fusion.10 = f32[8192]{0:T(1024)S(1)} fusion(f32[4097]{0:T(1024)S(1)} %pad_maximum_fusion.5, s32[8192]{0:T(1024)S(1)} %broadcast_clamp_fusion), kind=kCustom, calls=%fused_computation.10 | custom fusion | bytes 98304 | tf_op jit(solution)/shard_map/gather | solution.py:187
  834.5 30.7 %fusion.1 = bf16[512,16,1024]{2,0,1:T(8,128)(2,1)S(1)} fusion(f32[512,16,1024]{2,1,0:T(8,128)} %bitcast.217, f32[512,16]{0,1:T(8,128)S(1)} %copy.111), kind=kLoop, calls=%fused_computation.22 | loop fusion | flops 16777216 | bytes 50364416 | tf_op jit(solution)/shard_map/convert_element_type | solution.py:187
  865.2 401.7 %all_to_all.21 = bf16[512,16,1024]{2,0,1:T(8,128)(2,1)} all-to-all(bf16[512,16,1024]{2,0,1:T(8,128)(2,1)S(1)} %fusion.1), channel_id=1, replica_groups=mesh['ex'=16,'tp'=2] {'ex'}, dimensions={1} | all-to-all | bytes 33554432 | tf_op jit(solution)/shard_map/all_to_all | solution.py:188
  1266.9 19.8 %multiply_convert_fusion = (bf16[512,16,256]{2,0,1:T(8,128)(2,1)}, bf16[512,16,256]{2,0,1:T(8,128)(2,1)S(1)}) fusion(f32[512,16,256]{2,0,1:T(8,128)} %fusion.62, f32[512,16,256]{2,0,1:T(8,128)} %get-tuple-element.132, bf16[512,16,1024]{2,0,1:T(8,128)(2,1)} %all_to_all.21, bf16[1,256,1024]{2,1,0:T(8,128)(2,1)S(1)} %copy-done.42), kind=kOutput, calls=%fused_computation.32 | convolution fusion | flops 4322230272 | bytes 42467328 | tf_op jit(solution)/shard_map/cnd,fd->cnf/dot_general | solution.py:189
  1286.7 13.2 fusion.60
  1299.9 18.2 add_convert_fusion
  1318.2 24.7 %reduce-scatter.5.cloned.1.call-done = bf16[256,16,1024]{2,0,1:T(8,128)(2,1)} async-done(((bf16[512,16,1024]{2,0,1:T(8,128)(2,1)}), bf16[256,16,1024]{2,0,1:T(8,128)(2,1)}) %reduce-scatter.5.cloned.1.call-update) | async-done | bytes 8388624 | tf_op jit(solution)/shard_map/reduce_scatter | solution.py:202
  1342.9 6.9 all-to-all-start.3
  1352.2 156.7 %all-to-all-done.3 = bf16[256,16,1024]{2,0,1:T(8,128)(2,1)} async-done(((bf16[256,16,1024]{2,0,1:T(8,128)(2,1)}), bf16[256,16,1024]{2,0,1:T(8,128)(2,1)}, u32[]{:S(2)}, u32[]{:S(2)}) %all-to-all-start.3) | async-done | bytes 8388640 | tf_op jit(solution)/shard_map/all_to_all | solution.py:211
  1508.9 11.3 copy.113
  1520.2 8.2 gather_fusion.18
  1528.4 8.0 gather_fusion.17
  1536.4 8.0 gather_fusion.16
  1544.3 7.9 gather_fusion.15
  1552.3 8.0 gather_fusion.14
  1560.2 8.4 gather_fusion.13
  1568.7 8.0 gather_fusion.12
  1576.7 7.9 gather_fusion.11
  1590.0 6.2 add_convert_fusion.4
  1596.2 45.6 %all-reduce.12.cloned.1.call-done = bf16[512,1024]{1,0:T(8,128)(2,1)} async-done(((bf16[512,1024]{1,0:T(8,128)(2,1)}), bf16[512,1024]{1,0:T(8,128)(2,1)}) %all-reduce.12.cloned.1.call-update) | async-done | bytes 1048592 | tf_op jit(solution)/shard_map/psum | solution.py:217
  1654.8 15.6 fusion.41
  1670.4 15.9 fusion.39
  1692.5 12.5 convolution_bitcast_fusion.1
  1711.8 13.0 convolution_bitcast_fusion
  1724.8 10.2 convolution_bitcast_fusion.2
  1737.5 78.4 %all-reduce.2 = (bf16[1024]{0:T(1024)(128)(2,1)S(1)}, bf16[1024]{0:T(1024)(128)(2,1)S(1)}, bf16[1024,16]{0,1:T(8,128)(2,1)S(1)}) all-reduce(bf16[1024]{0:T(1024)(128)(2,1)S(1)} %get-tuple-element.55, bf16[1024]{0:T(1024)(128)(2,1)S(1)} %copy-done.87, bf16[1024,16]{0,1:T(8,128)(2,1)S(1)} %copy-done.52), channel_id=1, replica_groups=mesh['ex'=16,'tp'=2] {'ex'}, use_global_device_ids=true, to_apply=%region_32.33 | all-reduce | flops 18432 | bytes 73728 | tf_op jit(solution)/shard_map/psum | solution.py:292
  1822.2 50.1 %all-reduce.14.cloned.1.call-done = (bf16[1024,512]{1,0:T(8,128)(2,1)}, bf16[1024,256]{1,0:T(8,128)(2,1)}, bf16[1024,256]{1,0:T(8,128)(2,1)}, bf16[512,1024]{1,0:T(8,128)(2,1)}) async-done(((bf16[1024,512]{1,0:T(8,128)(2,1)}, bf16[1024,256]{1,0:T(8,128)(2,1)}, bf16[1024,256]{1,0:T(8,128)(2,1)}, bf16[512,1024]{1,0:T(8,128)(2,1)}), (bf16[1024,512]{1,0:T(8,128)(2,1)}, bf16[1024,256]{1,0:T(8,128)(2,1)}, ...) | async-done | bytes 3145744 | tf_op jit(solution)/shard_map/psum | solution.py:288
  (346 shorter events, 91.6 us)
Async XLA Ops:
  7.2 14.4 copy-start
  7.2 40.6 %all-reduce.10.cloned.1.call-start = ((), (), s32[]{:S(2)}) async-start(), calls=%async_computation.6 | async-start | bytes 4194304 | tf_op jit(solution)/shard_map/psum | solution.py:124
  23.7 514.8 %reduce-scatter.3.cloned.1.call-start = ((), (), s32[]{:S(2)}) async-start(), calls=%async_computation.7 | async-start | bytes 25165824 | tf_op jit(solution)/shard_map/reduce_scatter | solution.py:152
  102.2 376.3 %copy-start.32 = (bf16[1,1024,256]{2,1,0:T(8,128)(2,1)S(1)}, bf16[1,1024,256]{2,1,0:T(8,128)(2,1)}, u32[]{:S(2)}) copy-start(bf16[1,1024,256]{2,1,0:T(8,128)(2,1)} %param.23) | copy-start | bytes 1572868
  485.3 18.1 copy-start.41
  538.5 166.0 %all-to-all-start.1 = ((bf16[256,16,1024]{2,0,1:T(8,128)(2,1)}), bf16[256,16,1024]{2,0,1:T(8,128)(2,1)}, u32[]{:S(2)}, u32[]{:S(2)}) async-start(bf16[256,16,1024]{2,0,1:T(8,128)(2,1)} %reduce-scatter.3.cloned.1.call-done), calls=%async_computation.2 | async-start | bytes 16777216 | tf_op jit(solution)/shard_map/all_to_all | solution.py:160
  545.4 797.5 %reduce-scatter.5.cloned.1.call-start = ((), (), s32[]{:S(2)}) async-start(), calls=%async_computation.8 | async-start | bytes 25165824 | tf_op jit(solution)/shard_map/reduce_scatter | solution.py:202
  547.5 44.7 %copy-start.48 = (s32[512,8]{0,1:T(8,128)S(1)}, s32[512,8]{0,1:T(8,128)}, u32[]{:S(2)}) copy-start(s32[512,8]{0,1:T(8,128)} %param.26) | copy-start | bytes 49156
  547.5 45.1 %copy-start.43 = (f32[1024,16]{0,1:T(8,128)S(1)}, f32[1024,16]{0,1:T(8,128)}, u32[]{:S(2)}) copy-start(f32[1024,16]{0,1:T(8,128)} %param.22) | copy-start | bytes 196612
  547.5 45.1 %copy-start.56 = (f32[1024]{0:T(1024)S(1)}, f32[1024]{0:T(1024)}, u32[]{:S(2)}) copy-start(f32[1024]{0:T(1024)} %param.21) | copy-start | bytes 12292
  547.5 45.1 %copy-start.59 = (f32[512]{0:T(512)S(1)}, f32[512]{0:T(512)}, u32[]{:S(2)}) copy-start(f32[512]{0:T(512)} %copy-done.58) | copy-start | bytes 6148
  592.2 123.6 %copy-start.73 = (s32[1024]{0:T(1024)}, s32[1024]{0:T(1024)S(1)}, u32[]{:S(2)}) copy-start(s32[1024]{0:T(1024)S(1)} %pad_clamp_fusion) | copy-start | bytes 12292
  592.2 179.0 %copy-start.71 = (s32[1024]{0:T(1024)}, s32[1024]{0:T(1024)S(1)}, u32[]{:S(2)}) copy-start(s32[1024]{0:T(1024)S(1)} %pad_clamp_fusion.7) | copy-start | bytes 12292
  592.2 130.7 %copy-start.75 = (s32[1024]{0:T(1024)}, s32[1024]{0:T(1024)S(1)}, u32[]{:S(2)}) copy-start(s32[1024]{0:T(1024)S(1)} %pad_clamp_fusion.1) | copy-start | bytes 12292
  592.3 138.5 %copy-start.77 = (s32[1024]{0:T(1024)}, s32[1024]{0:T(1024)S(1)}, u32[]{:S(2)}) copy-start(s32[1024]{0:T(1024)S(1)} %pad_clamp_fusion.2) | copy-start | bytes 12292
  592.3 146.8 %copy-start.79 = (s32[1024]{0:T(1024)}, s32[1024]{0:T(1024)S(1)}, u32[]{:S(2)}) copy-start(s32[1024]{0:T(1024)S(1)} %pad_clamp_fusion.3) | copy-start | bytes 12292
  592.3 154.7 %copy-start.81 = (s32[1024]{0:T(1024)}, s32[1024]{0:T(1024)S(1)}, u32[]{:S(2)}) copy-start(s32[1024]{0:T(1024)S(1)} %pad_clamp_fusion.4) | copy-start | bytes 12292
  592.3 162.6 %copy-start.83 = (s32[1024]{0:T(1024)}, s32[1024]{0:T(1024)S(1)}, u32[]{:S(2)}) copy-start(s32[1024]{0:T(1024)S(1)} %pad_clamp_fusion.5) | copy-start | bytes 12292
  592.4 170.5 %copy-start.85 = (s32[1024]{0:T(1024)}, s32[1024]{0:T(1024)S(1)}, u32[]{:S(2)}) copy-start(s32[1024]{0:T(1024)S(1)} %pad_clamp_fusion.6) | copy-start | bytes 12292
  592.4 186.7 %copy-start.88 = (pred[512]{0:T(512)(128)(4,1)}, pred[512]{0:T(512)(128)(4,1)S(1)}, u32[]{:S(2)}) copy-start(pred[512]{0:T(512)(128)(4,1)S(1)} %get-tuple-element.75) | copy-start | bytes 1540
  592.5 186.7 %copy-start.90 = (pred[512]{0:T(512)(128)(4,1)}, pred[512]{0:T(512)(128)(4,1)S(1)}, u32[]{:S(2)}) copy-start(pred[512]{0:T(512)(128)(4,1)S(1)} %get-tuple-element.76) | copy-start | bytes 1540
  592.5 186.7 %copy-start.92 = (pred[512]{0:T(512)(128)(4,1)}, pred[512]{0:T(512)(128)(4,1)S(1)}, u32[]{:S(2)}) copy-start(pred[512]{0:T(512)(128)(4,1)S(1)} %get-tuple-element.77) | copy-start | bytes 1540
  592.5 186.7 %copy-start.94 = (pred[512]{0:T(512)(128)(4,1)}, pred[512]{0:T(512)(128)(4,1)S(1)}, u32[]{:S(2)}) copy-start(pred[512]{0:T(512)(128)(4,1)S(1)} %get-tuple-element.78) | copy-start | bytes 1540
  592.5 186.7 %copy-start.96 = (pred[512]{0:T(512)(128)(4,1)}, pred[512]{0:T(512)(128)(4,1)S(1)}, u32[]{:S(2)}) copy-start(pred[512]{0:T(512)(128)(4,1)S(1)} %get-tuple-element.79) | copy-start | bytes 1540
  592.5 186.7 %copy-start.98 = (pred[512]{0:T(512)(128)(4,1)}, pred[512]{0:T(512)(128)(4,1)S(1)}, u32[]{:S(2)}) copy-start(pred[512]{0:T(512)(128)(4,1)S(1)} %get-tuple-element.80) | copy-start | bytes 1540
  592.5 186.7 %copy-start.100 = (pred[512]{0:T(512)(128)(4,1)}, pred[512]{0:T(512)(128)(4,1)S(1)}, u32[]{:S(2)}) copy-start(pred[512]{0:T(512)(128)(4,1)S(1)} %get-tuple-element.81) | copy-start | bytes 1540
  592.5 186.7 %copy-start.102 = (pred[512]{0:T(512)(128)(4,1)}, pred[512]{0:T(512)(128)(4,1)S(1)}, u32[]{:S(2)}) copy-start(pred[512]{0:T(512)(128)(4,1)S(1)} %get-tuple-element.82) | copy-start | bytes 1540
  723.0 56.2 %copy-start.13 = (bf16[512,1024]{1,0:T(8,128)(2,1)}, bf16[512,1024]{1,0:T(8,128)(2,1)S(1)}, u32[]{:S(2)}) copy-start(bf16[512,1024]{1,0:T(8,128)(2,1)S(1)} %gather_fusion.8) | copy-start | bytes 3145732
  730.8 48.4 %copy-start.14 = (bf16[512,1024]{1,0:T(8,128)(2,1)}, bf16[512,1024]{1,0:T(8,128)(2,1)S(1)}, u32[]{:S(2)}) copy-start(bf16[512,1024]{1,0:T(8,128)(2,1)S(1)} %gather_fusion.7) | copy-start | bytes 3145732
  865.2 401.7 %copy-start.42 = (bf16[1,256,1024]{2,1,0:T(8,128)(2,1)S(1)}, bf16[1,256,1024]{2,1,0:T(8,128)(2,1)}, u32[]{:S(2)}) copy-start(bf16[1,256,1024]{2,1,0:T(8,128)(2,1)} %param.25) | copy-start | bytes 1572868
  1266.9 19.8 %copy-start.33 = (bf16[1,1024,256]{2,1,0:T(8,128)(2,1)S(1)}, bf16[1,1024,256]{2,1,0:T(8,128)(2,1)}, u32[]{:S(2)}) copy-start(bf16[1,1024,256]{2,1,0:T(8,128)(2,1)} %param.23) | copy-start | bytes 1572868
  1318.1 31.9 %copy-start.64 = (f32[4,2,512]{2,1,0:T(2,128)S(1)}, f32[4,2,512]{2,1,0:T(2,128)}, u32[]{:S(2)}) copy-start(f32[4,2,512]{2,1,0:T(2,128)} %copy-done.63) | copy-start | bytes 49156
  1318.1 31.9 %copy-start.66 = (f32[4,2,512]{2,1,0:T(2,128)S(1)}, f32[4,2,512]{2,1,0:T(2,128)}, u32[]{:S(2)}) copy-start(f32[4,2,512]{2,1,0:T(2,128)} %copy-done.65) | copy-start | bytes 49156
  1318.2 31.9 %copy-start.46 = (f32[512,8]{0,1:T(8,128)S(1)}, f32[512,8]{0,1:T(8,128)}, u32[]{:S(2)}) copy-start(f32[512,8]{0,1:T(8,128)} %copy-done.45) | copy-start | bytes 49156
  1318.2 31.9 %copy-start.62 = (bf16[512,8]{0,1:T(8,128)(2,1)S(1)}, bf16[512,8]{0,1:T(8,128)(2,1)}, u32[]{:S(2)}) copy-start(bf16[512,8]{0,1:T(8,128)(2,1)} %copy-done.61) | copy-start | bytes 24580
  1318.2 31.9 %copy-start.104 = (f32[512]{0:T(512)S(1)}, f32[512]{0:T(512)}, u32[]{:S(2)}) copy-start(f32[512]{0:T(512)} %get-tuple-element.92) | copy-start | bytes 6148
  1318.2 32.0 %copy-start.49 = (s32[512,8]{0,1:T(8,128)S(1)}, s32[512,8]{0,1:T(8,128)}, u32[]{:S(2)}) copy-start(s32[512,8]{0,1:T(8,128)} %param.26) | copy-start | bytes 49156
  1318.2 32.0 %copy-start.3 = (f32[512,1024]{1,0:T(8,128)S(1)}, f32[512,1024]{1,0:T(8,128)}, u32[]{:S(2)}) copy-start(f32[512,1024]{1,0:T(8,128)} %copy-done.2) | copy-start | bytes 6291460
  1318.2 32.0 %copy-start.57 = (f32[1024]{0:T(1024)S(1)}, f32[1024]{0:T(1024)}, u32[]{:S(2)}) copy-start(f32[1024]{0:T(1024)} %param.21) | copy-start | bytes 12292
  1318.2 32.0 %copy-start.60 = (f32[512]{0:T(512)S(1)}, f32[512]{0:T(512)}, u32[]{:S(2)}) copy-start(f32[512]{0:T(512)} %copy-done.58) | copy-start | bytes 6148
  1342.9 166.0 %all-to-all-start.3 = ((bf16[256,16,1024]{2,0,1:T(8,128)(2,1)}), bf16[256,16,1024]{2,0,1:T(8,128)(2,1)}, u32[]{:S(2)}, u32[]{:S(2)}) async-start(bf16[256,16,1024]{2,0,1:T(8,128)(2,1)} %reduce-scatter.5.cloned.1.call-done), calls=%async_computation.5 | async-start | bytes 16777216 | tf_op jit(solution)/shard_map/all_to_all | solution.py:211
  1349.8 292.0 %all-reduce.12.cloned.1.call-start = ((), (), s32[]{:S(2)}) async-start(), calls=%async_computation.9 | async-start | bytes 2097152 | tf_op jit(solution)/shard_map/psum | solution.py:217
  1352.2 168.0 %copy-start.74 = (s32[1024]{0:T(1024)S(1)}, s32[1024]{0:T(1024)}, u32[]{:S(2)}) copy-start(s32[1024]{0:T(1024)} %copy-done.73) | copy-start | bytes 12292
  1589.9 145.1 %all-reduce.16.cloned.1.call-start = ((), (), s32[]{:S(2)}) async-start(), calls=%async_computation.11 | async-start | bytes 4194304 | tf_op jit(solution)/shard_map/psum | solution.py:177
  1590.0 51.8 %copy-start.44 = (f32[1024,16]{0,1:T(8,128)S(1)}, f32[1024,16]{0,1:T(8,128)}, u32[]{:S(2)}) copy-start(f32[1024,16]{0,1:T(8,128)} %param.22) | copy-start | bytes 196612
  1670.4 15.9 copy-start.22
  1670.4 15.9 copy-start.24
  1692.5 179.9 %all-reduce.14.cloned.1.call-start = ((), (), s32[]{:S(2)}) async-start(), calls=%async_computation.10 | async-start | bytes 6291456 | tf_op jit(solution)/shard_map/psum | solution.py:288
  (69 other events, 341.0 us)
Sparse Core Ops, SparseCore 0:
  23.8 23.9 all-reduce.9
  513.9 24.5 reduce-scatter.2
  1318.3 24.6 reduce-scatter.4
  1590.0 51.7 all-reduce.11
  1692.6 22.4 all-reduce.15
  1722.7 149.6 all-reduce.13
where the time goes:
time: 1900 us; the launch traced here: 1890 us
  blocking collectives  853 us (45%)
  waiting for transfers between devices  411 us (22%)
  local copies, waits for them, and re-layouts  324 us (17%)
  matrix products  188 us (10%)
  other arithmetic  78.3 us (4%)
    all_to_all x1, blocking collectives, shards(): lax.all_to_all(grad_send, 'ex', split_axis=1, concat_axis=1, tiled=True)  402 us
    all_to_all x1, blocking collectives, shards(): lax.all_to_all(padded[table // topk], 'ex', split_axis=1, concat_axis=1,...  371 us
    all_to_all x1, waiting for transfers between devices, shards(): lax.all_to_all(input_sum, 'ex', split_axis=1, concat_axis=1, tiled=True)  157 us
    all_to_all x1, waiting for transfers between devices, shards(): lax.all_to_all(expert_sum, 'ex', split_axis=1, concat_axis=1, tiled=True)  108 us
    psum x1, blocking collectives, shards(): lax.psum(grad_gain_one.astype(jnp.bfloat16), 'ex').astype(jnp.float32)  78.4 us
    gather x8, local copies, waits for them, and re-layouts, shards(): picked = flat_input[flat_place[:, choice_index]].astype(jnp.float32)  64.3 us
    gather x8, local copies, waits for them, and re-layouts, shards(): picked = flat_returned[flat_place[:, choice_index]].astype(jnp.float32)  63.3 us
    gather x2, local copies, waits for them, and re-layouts, shards(): padded[table // topk]  50.8 us
  transfers between devices with their start and end apart: 8, of which 7 were waited for; matrix products, arithmetic and copies ran while one was open for 7% of the time, Pallas kernels for 0%

commit v1 on v0

v1 whole, which is shorter than its diff:
```python
import jax
import jax.numpy as jnp
from jax import lax
from jax.sharding import PartitionSpec as P

QUERY_HEADS = 16
KEY_VALUE_HEADS = 8
HEAD_SIZE = 64


EPS = 1e-06
THETA = 10000.0
NEGATIVE = -1e30
HIGH = lax.Precision.HIGHEST


def norm_scale(value_rows):
    return lax.rsqrt(jnp.mean(value_rows * value_rows, axis=-1, keepdims=True) + EPS)


def norm_backward(value_rows, scale, gain, grad):
    weighted = grad * gain
    inner = jnp.mean(weighted * value_rows, axis=-1, keepdims=True)
    grad_input = scale * weighted - value_rows * scale * scale * scale * inner
    grad_gain = jnp.sum(grad * value_rows * scale, axis=0)
    return (grad_input, grad_gain)


def rope_tables(length, split, width):
    index = jnp.arange(length, dtype=jnp.int32)
    second = index >= split
    place = jnp.where(second, index - split, index).astype(jnp.float32)
    freq = THETA ** (-(jnp.arange(width // 2, dtype=jnp.float32) * 2.0 / width))
    angle = place[:, None] * freq[None, :]
    return (jnp.cos(angle)[:, None, None, :], jnp.sin(angle)[:, None, None, :], second)


def apply_rotary(value_rows, cosine_table, sine_table):
    middle = value_rows.shape[-1] // 2
    front = value_rows[..., :middle]
    back = value_rows[..., middle:]
    return jnp.concatenate(
        [front * cosine_table - back * sine_table, back * cosine_table + front * sine_table],
        axis=-1,
    )


def rotate_back(grad, cosine_table, sine_table):
    middle = grad.shape[-1] // 2
    front = grad[..., :middle]
    back = grad[..., middle:]
    return jnp.concatenate(
        [front * cosine_table + back * sine_table, back * cosine_table - front * sine_table],
        axis=-1,
    )


def block_scores(query_block, key_rows, offset, second, factor):
    raw = jnp.einsum("qkgd,skd->kgqs", query_block, key_rows, preferred_element_type=jnp.float32)
    height = query_block.shape[0]
    row_index = offset + jnp.arange(height, dtype=jnp.int32)
    col_index = jnp.arange(key_rows.shape[0], dtype=jnp.int32)
    allowed = (col_index[None, :] <= row_index[:, None]) & (second[None, :] == second[:, None])
    return jnp.where(allowed, raw * factor, NEGATIVE)


BITS = (1, 2)


def swap(rows):
    return lax.ppermute(rows, "tp", [(0, 1), (1, 0)])


def tp_sum(part):
    if lax.axis_size("tp") == 2:
        return part + swap(part)
    return lax.psum(part, "tp")


def own_first(rows):
    if lax.axis_size("tp") == 2:
        half = rows.shape[0] // 2
        place = lax.axis_index("tp")
        own = lax.dynamic_slice_in_dim(rows, place * half, half, 0)
        other = lax.dynamic_slice_in_dim(rows, (1 - place) * half, half, 0)
        return (own, jnp.concatenate([own, other], axis=0))
    share = rows.shape[0] // lax.axis_size("tp")
    own = lax.dynamic_slice_in_dim(rows, lax.axis_index("tp") * share, share, 0)
    return (own, rows)


def flip_columns(values):
    if lax.axis_size("tp") == 2:
        half = values.shape[-1] // 2
        turned = jnp.concatenate([values[..., half:], values[..., :half]], axis=-1)
        return jnp.where(lax.axis_index("tp") == 0, values, turned)
    return values


def join_halves(own):
    if lax.axis_size("tp") == 2:
        return jnp.concatenate([own, swap(own)], axis=0)
    return lax.all_gather(own, "tp", axis=0, tiled=True)


def sum_halves(part):
    if lax.axis_size("tp") == 2:
        half = part.shape[0] // 2
        return part[:half] + swap(part[half:])
    return lax.psum_scatter(part, "tp", scatter_dimension=0, tiled=True)


def absolute_rows(own):
    if lax.axis_size("tp") == 2:
        other = swap(own)
        first = lax.axis_index("tp") == 0
        return jnp.concatenate(
            [jnp.where(first, own, other), jnp.where(first, other, own)], axis=0
        )
    return lax.all_gather(own, "tp", axis=0, tiled=True)


def group_pairs(turn):
    ex = lax.axis_size("ex")
    tp = lax.axis_size("tp")
    pairs = []
    for place in range(ex):
        for core in range(tp):
            bit = BITS[(turn + core) % 2]
            pairs.append((place * tp + core, (place ^ bit) * tp + core))
    return pairs


def group_swap(value_rows, turn):
    return lax.ppermute(value_rows, ("ex", "tp"), group_pairs(turn))


def line_shift(value_rows, step):
    ex = lax.axis_size("ex")
    moved = 4 * step
    return lax.ppermute(value_rows, "ex", [(place, (place - moved) % ex) for place in range(ex)])


def group_gather(value_rows):
    for turn in range(2):
        value_rows = jnp.concatenate([value_rows, group_swap(value_rows, turn)], axis=-1)
    return value_rows


def group_scatter(value_rows):
    for turn in (1, 0):
        half = value_rows.shape[-1] // 2
        sent = group_swap(value_rows[..., half:].astype(jnp.bfloat16), turn)
        value_rows = value_rows[..., :half] + sent.astype(jnp.float32)
    return value_rows


def group_bit(turn):
    bit = jnp.where((lax.axis_index("tp") + turn) % 2 == 0, BITS[0], BITS[1])
    return ((lax.axis_index("ex") & bit) != 0).astype(jnp.int32)


def everywhere_sum(value_rows):
    planes = lax.axis_size("ex") // 4
    for turn in (1, 0):
        half = value_rows.shape[0] // 2
        bit = group_bit(turn)
        kept = lax.dynamic_slice_in_dim(value_rows, bit * half, half, 0)
        sent = lax.dynamic_slice_in_dim(value_rows, (1 - bit) * half, half, 0)
        sent = group_swap(sent.astype(jnp.bfloat16), turn)
        value_rows = kept + sent.astype(jnp.float32)
    share = value_rows.shape[0] // planes
    plane = lax.axis_index("ex") // 4
    low = value_rows.astype(jnp.bfloat16)
    total = lax.dynamic_slice_in_dim(value_rows, plane * share, share, 0)
    for step in range(1, planes):
        target = lax.rem(plane + planes - step, planes)
        piece = lax.dynamic_slice_in_dim(low, target * share, share, 0)
        total = total + line_shift(piece, step).astype(jnp.float32)
    total = total.astype(jnp.bfloat16)
    value_rows = lax.dynamic_update_slice_in_dim(low, total, plane * share, 0)
    for step in range(1, planes):
        source = lax.rem(plane + step, planes)
        value_rows = lax.dynamic_update_slice_in_dim(
            value_rows, line_shift(total, step), source * share, 0
        )
    for turn in range(2):
        first = group_bit(turn) == 0
        other = group_swap(value_rows, turn)
        value_rows = jnp.concatenate(
            [jnp.where(first, value_rows, other), jnp.where(first, other, value_rows)], axis=0
        )
    return value_rows


def shards(
    tokens,
    cotangent,
    gain_one,
    w_query,
    key_weight,
    value_weight,
    w_out,
    gain_two,
    router,
    w_gate,
    w_up,
    w_down,
    expert_ids,
    leading_sequence_length,
):
    length = tokens.shape[0]
    width = tokens.shape[1]
    experts = router.shape[1]
    planes = lax.axis_size("ex") // 4
    plane = lax.axis_index("ex") // 4
    member = lax.axis_index("ex") % 4
    odd = lax.axis_index("tp") % 2
    query_group = QUERY_HEADS // KEY_VALUE_HEADS
    kv_local = key_weight.shape[1] // HEAD_SIZE
    q_width = w_query.shape[1]
    units = w_gate.shape[2]
    factor = float(HEAD_SIZE) ** (-0.5)
    low = jnp.bfloat16
    f32 = jnp.float32

    expert_weights = group_gather(jnp.stack([w_gate[0], w_up[0], w_down[0].T], axis=0))
    gate_w = expert_weights[0]
    up_w = expert_weights[1]
    down_w = expert_weights[2]
    grad_held = [own_first(cotangent)]
    for step in range(1, planes):
        arrived = line_shift(grad_held[-1][0], 1)
        grad_held.append((arrived, join_halves(arrived)))

    x_full = tokens.astype(f32)
    scale_one = norm_scale(x_full)
    normed_one = (x_full * scale_one * gain_one).astype(low)
    cosine_table, sine_table, second = rope_tables(length, leading_sequence_length[0], HEAD_SIZE)
    query_pre = jnp.dot(normed_one, w_query, preferred_element_type=f32).reshape(
        length, kv_local, query_group, HEAD_SIZE
    )
    query_rows = apply_rotary(query_pre, cosine_table, sine_table).astype(low)
    key_pre = jnp.dot(normed_one, key_weight, preferred_element_type=f32).reshape(
        length, kv_local, 1, HEAD_SIZE
    )
    key_rows = apply_rotary(key_pre, cosine_table, sine_table).astype(low)[:, :, 0, :]
    value_rows = (
        jnp.dot(normed_one, value_weight, preferred_element_type=f32)
        .astype(low)
        .reshape(length, kv_local, HEAD_SIZE)
    )
    scores = block_scores(query_rows, key_rows, 0, second, factor)
    largest = jnp.max(scores, axis=-1, keepdims=True)
    weights = jnp.exp(scores - largest)
    total = jnp.sum(weights, axis=-1, keepdims=True)
    probs = (weights / total).astype(low)
    log_totals = (largest + jnp.log(total))[..., 0]
    heads = (
        jnp.einsum("kgqs,skd->qkgd", probs, value_rows, preferred_element_type=f32)
        .astype(low)
        .reshape(length, q_width)
    )
    mixed = x_full + tp_sum(jnp.dot(heads, w_out, preferred_element_type=f32))
    scale_two = norm_scale(mixed)
    normed_two = mixed * scale_two * gain_two
    routed = normed_two.astype(low)
    logits = lax.dot_general(router, normed_two, (((0,), (1,)), ((), ())), precision=HIGH)
    expert_iota = jnp.arange(experts, dtype=jnp.int32)
    chosen = jnp.any(expert_ids.T[None, :, :] == expert_iota[:, None, None], axis=1)
    masked = jnp.where(chosen, logits, NEGATIVE)
    gate_weights = jnp.where(chosen, jnp.exp(masked - jnp.max(masked, axis=0, keepdims=True)), 0.0)
    gates = gate_weights / jnp.sum(gate_weights, axis=0, keepdims=True)

    gates_high = gates.astype(low)
    gates_rest = (gates - gates_high.astype(f32)).astype(low)
    extra = jnp.concatenate([gates_high, gates_rest], axis=1)
    extra = jnp.pad(extra, ((0, 0), (0, width - extra.shape[1])))
    own_routed, own_block = own_first(routed)
    payload = jnp.concatenate([own_routed, extra], axis=0)
    share = own_routed.shape[0]
    blocks = [(own_block, gates)]
    for step in range(1, planes):
        payload = line_shift(payload, 1)
        sent_gates = payload[share:].astype(f32)
        blocks.append(
            (
                join_halves(payload[:share]),
                sent_gates[:, :length] + sent_gates[:, length : 2 * length],
            )
        )

    slots = jnp.arange(4, dtype=jnp.int32)
    flipped = (slots % 2) * 2 + slots // 2
    slot_member = jnp.where(odd == 1, flipped, slots) ^ member
    slot_expert = plane * 4 + slot_member
    placed = (expert_iota[:, None] == slot_expert[None, :]).astype(f32)

    def expert_block(rows, grads, block_gates):
        pre_gate = jnp.dot(rows, gate_w, preferred_element_type=f32)
        pre_up = jnp.dot(rows, up_w, preferred_element_type=f32)
        grad_plain = jnp.dot(grads, down_w, preferred_element_type=f32)
        slot_gates = jnp.sum(
            placed[:, :, None] * flip_columns(block_gates)[:, None, :], axis=0
        ).T
        wide_gates = jnp.broadcast_to(slot_gates[:, :, None], (length, 4, units)).reshape(
            length, 4 * units
        )
        sigmoid = jax.nn.sigmoid(pre_gate)
        activated = pre_gate * sigmoid
        hidden = activated * pre_up
        gate_part = jnp.sum((hidden * grad_plain).reshape(length, 4, units), axis=-1).T
        gate_part = flip_columns(jnp.sum(placed[:, :, None] * gate_part[None, :, :], axis=1))
        hidden = (hidden * wide_gates).astype(low)
        grad_hidden = grad_plain * wide_gates
        grad_pre_gate = (
            grad_hidden * pre_up * sigmoid * (1.0 + pre_gate * (1.0 - sigmoid))
        ).astype(low)
        grad_pre_up = (grad_hidden * activated).astype(low)
        back = lax.dot_general(
            grad_pre_gate, gate_w, (((1,), (1,)), ((), ())), preferred_element_type=f32
        ) + lax.dot_general(
            grad_pre_up, up_w, (((1,), (1,)), ((), ())), preferred_element_type=f32
        )
        front = lax.dot_general(
            hidden, down_w, (((1,), (1,)), ((), ())), preferred_element_type=f32
        )
        return (back.astype(low), front.astype(low), gate_part, hidden, grad_pre_gate, grad_pre_up)

    results = [
        expert_block(blocks[step][0], grad_held[step][1], blocks[step][1])
        for step in range(planes)
    ]

    def packed_back(step):
        back, front, gate_part, *unused = results[step]
        part_high = gate_part.astype(low)
        part_rest = (gate_part - part_high.astype(f32)).astype(low)
        rest = jnp.concatenate([part_high, part_rest], axis=1)
        rest = jnp.pad(rest, ((0, 0), (0, width - rest.shape[1])))
        return jnp.concatenate([sum_halves(back), rest], axis=0)

    def line_sum(pieces):
        running = None
        for step in range(1, planes):
            piece = pieces(step)
            running = piece if running is None else running + piece
            running = line_shift(running, 1)
        last = pieces(0)
        return last if running is None else running + last

    back_sum = line_sum(packed_back)
    grad_moe = absolute_rows(back_sum[:share]).astype(f32)
    gate_sum = back_sum[share:].astype(f32)
    gate_grads = tp_sum(gate_sum[:, :length] + gate_sum[:, length : 2 * length])

    grad_out = cotangent.astype(f32)
    grad_logits = gates * (gate_grads - jnp.sum(gates * gate_grads, axis=0, keepdims=True))
    grad_router = lax.dot_general(
        normed_two, grad_logits, (((0,), (1,)), ((), ())), precision=HIGH
    )
    grad_normed_two = grad_moe + lax.dot_general(
        grad_logits, router, (((0,), (1,)), ((), ())), precision=HIGH
    )
    grad_mixed_norm, grad_gain_two = norm_backward(mixed, scale_two, gain_two, grad_normed_two)
    grad_mixed = grad_out + grad_mixed_norm
    grad_attended = grad_mixed.astype(low)

    def packed_front(step):
        return sum_halves(fronts[step])

    fronts = [results[step][1] for step in range(planes)]
    fronts = list(lax.optimization_barrier((*fronts, back_sum))[:planes])
    front_sum = line_sum(packed_front)
    output = (mixed + absolute_rows(front_sum).astype(f32)).astype(low)

    all_rows = jnp.concatenate([block[0] for block in blocks], axis=0)
    all_grads = jnp.concatenate([held[1] for held in grad_held], axis=0)
    all_hidden = jnp.concatenate([result[3] for result in results], axis=0)
    all_gate = jnp.concatenate([result[4] for result in results], axis=0)
    all_up = jnp.concatenate([result[5] for result in results], axis=0)

    def over_rows(left, right):
        return lax.dot_general(left, right, (((0,), (0,)), ((), ())), preferred_element_type=f32)

    expert_grads = group_scatter(
        jnp.stack(
            [
                over_rows(all_rows, all_gate),
                over_rows(all_rows, all_up),
                over_rows(all_grads, all_hidden),
            ],
            axis=0,
        )
    )

    grad_out_proj = over_rows(heads, grad_attended)
    grad_out_proj = everywhere_sum(grad_out_proj).astype(f32)
    grad_heads = jnp.einsum("td,hd->th", grad_attended, w_out, preferred_element_type=f32)
    grad_heads = grad_heads.astype(low).reshape(length, kv_local, query_group, HEAD_SIZE)
    scores = block_scores(query_rows, key_rows, 0, second, factor)
    probs = jnp.exp(scores - log_totals[..., None])
    probs_low = probs.astype(low)
    grad_probs = jnp.einsum("qkgd,skd->kgqs", grad_heads, value_rows, preferred_element_type=f32)
    inner = jnp.sum(probs * grad_probs, axis=-1, keepdims=True)
    grad_scores = (probs * (grad_probs - inner) * factor).astype(low)
    grad_queries = jnp.einsum("kgqs,skd->qkgd", grad_scores, key_rows, preferred_element_type=f32)
    grad_keys = jnp.einsum("kgqs,qkgd->skd", grad_scores, query_rows, preferred_element_type=f32)
    grad_values = jnp.einsum("kgqs,qkgd->skd", probs_low, grad_heads, preferred_element_type=f32)
    grad_queries = rotate_back(grad_queries, cosine_table, sine_table)
    grad_queries = grad_queries.astype(low).reshape(length, q_width)
    grad_keys_pre = (
        rotate_back(grad_keys[:, :, None, :], cosine_table, sine_table)
        .astype(low)
        .reshape(length, kv_local * HEAD_SIZE)
    )
    grad_values_low = grad_values.astype(low).reshape(length, kv_local * HEAD_SIZE)
    grad_three = jnp.concatenate([grad_queries, grad_keys_pre, grad_values_low], axis=1)
    three_weights = jnp.concatenate([w_query, key_weight, value_weight], axis=1)
    grad_normed_one = lax.dot_general(
        grad_three, three_weights, (((1,), (1,)), ((), ())), preferred_element_type=f32
    )
    grad_normed_one = tp_sum(grad_normed_one.astype(low)).astype(f32)
    weight_grads = everywhere_sum(over_rows(normed_one, grad_three)).astype(f32)
    grad_input_norm, grad_gain_one = norm_backward(x_full, scale_one, gain_one, grad_normed_one)
    grad_tokens = (grad_mixed + grad_input_norm).astype(low)
    grad_gain_one, grad_gain_two, grad_router = (
        lax.psum(grad_gain_one, "ex"),
        lax.psum(grad_gain_two, "ex"),
        lax.psum(grad_router, "ex"),
    )
    key_end = q_width + key_weight.shape[1]
    return (
        output,
        grad_tokens,
        grad_gain_one,
        weight_grads[:, :q_width],
        weight_grads[:, q_width:key_end],
        weight_grads[:, key_end:],
        grad_out_proj,
        grad_gain_two,
        grad_router,
        expert_grads[0][None],
        expert_grads[1][None],
        expert_grads[2].T[None],
    )


def solution(mesh):
    placed = (
        P("ex", None),
        P("ex", None),
        P(),
        P(None, "tp"),
        P(None, "tp"),
        P(None, "tp"),
        P("tp", None),
        P(),
        P(),
        P("ex", None, "tp"),
        P("ex", None, "tp"),
        P("ex", "tp", None),
        P("ex", None),
        P("ex"),
    )
    return jax.shard_map(
        shards,
        mesh=mesh,
        in_specs=placed,
        out_specs=(
            P("ex", None),
            P("ex", None),
            P(),
            P(None, "tp"),
            P(None, "tp"),
            P(None, "tp"),
            P("tp", None),
            P(),
            P(),
            P("ex", None, "tp"),
            P("ex", None, "tp"),
            P("ex", "tp", None),
        ),
        check_vma=False,
    )
```

time: 1900 us -> 582 us (0.31)
  blocking collectives: 853 us -> 39.7 us
  waiting for transfers between devices: 411 us -> 148 us
  local copies, waits for them, and re-layouts: 324 us -> 77.2 us
  starting transfers between devices: 14.2 us -> 78.4 us
  matrix products: 188 us -> 149 us
    all_to_all x2 -> x0, blocking collectives: 772 us -> none  [the longest x1 402 us: shards(): lax.all_to_all(grad_send, 'ex', split_axis=1, concat_axis=1, tiled=True)]
    gather x22 -> x0, local copies, waits for them, and re-layouts: 269 us -> none  [the longest x8 64.3 us: shards(): picked = flat_input[flat_place[:, choice_index]].astype(jnp.float32)]
    all_to_all x2 -> x0, waiting for transfers between devices: 265 us -> none  [the longest x1 157 us: shards(): lax.all_to_all(input_sum, 'ex', split_axis=1, concat_axis=1, tiled=True)]
    ppermute x0 -> x55, waiting for transfers between devices: none -> 148 us  [the longest x24 120 us: line_shift(): lax.ppermute(value_rows, 'ex', [(place, (place - moved) % ex) for place i...]
    psum x4 -> x1, waiting for transfers between devices: 97 us -> 0.01 us  [shards(): lax.psum(grad_router, 'ex')]
    ppermute x0 -> x55, starting transfers between devices: none -> 78.3 us  [the longest x24 63.9 us: line_shift(): lax.ppermute(value_rows, 'ex', [(place, (place - moved) % ex) for place i...]
    reduce_scatter x2 -> x0, waiting for transfers between devices: 49.4 us -> none  [the longest x1 24.7 us: shards(): lax.psum_scatter(jnp.einsum('cnf,fd->cnd', hidden, down_w, preferred_elem...]
    psum x2 -> x1, blocking collectives: 80.9 us -> 39.7 us  [shards(): lax.psum(grad_gain_one, 'ex')]
  transfers between devices with their start and end apart: 8 -> 56, of which waited for: 7 -> 20; matrix products, arithmetic and copies ran while one was open for 7% -> 29% of each run, Pallas kernels for 0% -> 0%
where the time goes in v1:
time: 582 us; the launch traced here: 574 us
  matrix products  149 us (26%)
  waiting for transfers between devices  148 us (25%)
  starting transfers between devices  78.4 us (13%)
  local copies, waits for them, and re-layouts  77.2 us (13%)
  other arithmetic  64.8 us (11%)
  blocking collectives  39.7 us (7%)
  between operations  17.5 us (3%)
    ppermute x24, waiting for transfers between devices, line_shift(): lax.ppermute(value_rows, 'ex', [(place, (place - moved) % ex) for place i...  120 us
    ppermute x24, starting transfers between devices, line_shift(): lax.ppermute(value_rows, 'ex', [(place, (place - moved) % ex) for place i...  63.9 us
    unnamed x248, local copies, waits for them, and re-layouts  46.2 us
    psum x1, blocking collectives, shards(): lax.psum(grad_gain_one, 'ex')  39.7 us
    ppermute x12, waiting for transfers between devices, group_swap(): return lax.ppermute(value_rows, ('ex', 'tp'), group_pairs(turn))  25.7 us
    dot_general x4, matrix products, expert_block(): grad_plain = jnp.dot(grads, down_w, preferred_element_type=f32)  22.5 us
    dot_general x5, matrix products, over_rows(): lax.dot_general(left, right, (((0,), (0,)), ((), ())), preferred_element_...  21 us
    dot_general x1, matrix products, shards(): jnp.einsum('kgqs,skd->qkgd', grad_scores, key_rows, preferred_element_typ...  16.2 us
  transfers between devices with their start and end apart: 56, of which 20 were waited for; matrix products, arithmetic and copies ran while one was open for 29% of the time, Pallas kernels for 0%

profile of v1, /device:TPU:0, one launch (start us, length us, event | category | flops | bytes accessed | tf_op | source)
XLA Modules:
  0.0 573.8 jit_solution(9331161901780426532)
XLA Ops:
  9.6 5.0 collective-permute-start.9
  33.9 13.3 %collective-permute-done.13 = bf16[256,1024]{1,0:T(8,128)(2,1)} collective-permute-done((bf16[256,1024]{1,0:T(8,128)(2,1)}, bf16[256,1024]{1,0:T(8,128)(2,1)}, u32[]{:S(2)}, u32[]{:S(2)}) %collective-permute-start.13) | collective-permute-done | bytes 524320 | tf_op jit(solution)/shard_map/ppermute | solution.py:141
  57.5 3.5 collective-permute-done.17
  72.6 4.1 collective-permute-start.3
  77.8 11.1 %collective-permute-done.3 = bf16[272,1024]{1,0:T(8,128)(2,1)S(1)} collective-permute-done((bf16[272,1024]{1,0:T(8,128)(2,1)S(1)}, bf16[272,1024]{1,0:T(8,128)(2,1)S(1)}, u32[]{:S(2)}, u32[]{:S(2)}) %collective-permute-start.3) | collective-permute-done | bytes 557088 | tf_op jit(solution)/shard_map/ppermute | solution.py:141
  90.1 4.0 collective-permute-start.5
  94.9 11.3 %collective-permute-done.5 = bf16[272,1024]{1,0:T(8,128)(2,1)S(1)} collective-permute-done((bf16[272,1024]{1,0:T(8,128)(2,1)S(1)}, bf16[272,1024]{1,0:T(8,128)(2,1)S(1)}, u32[]{:S(2)}, u32[]{:S(2)}) %collective-permute-start.5) | collective-permute-done | bytes 557088 | tf_op jit(solution)/shard_map/ppermute | solution.py:141
  106.4 4.3 collective-permute-start.7
  110.8 12.4 %collective-permute-done.7 = bf16[272,1024]{1,0:T(8,128)(2,1)S(1)} collective-permute-done((bf16[272,1024]{1,0:T(8,128)(2,1)S(1)}, bf16[272,1024]{1,0:T(8,128)(2,1)S(1)}, u32[]{:S(2)}, u32[]{:S(2)}) %collective-permute-start.7) | collective-permute-done | bytes 557088 | tf_op jit(solution)/shard_map/ppermute | solution.py:141
  128.1 4.1 pad_maximum_fusion.1
  135.5 4.5 multiply_multiply_fusion.10
  143.0 3.3 fusion.111
  146.3 3.6 fusion.112
  150.0 6.0 %multiply_multiply_fusion.9 = (f32[512,1024]{1,0:T(8,128)}, f32[512,1024]{1,0:T(8,128)}) fusion(f32[512,1024]{1,0:T(8,128)S(1)} %fusion.111, f32[512,1024]{1,0:T(8,128)S(1)} %fusion.112, bf16[3,1024,1024]{1,2,0:T(8,128)(2,1)} %copy-done.14, bf16[256,1024]{1,0:T(8,128)(2,1)} %collective-permute-done.10, bf16[256,1024]{1,0:T(8,128)(2,1)} %collective-permute-done.9), kind=kOutput, calls=%fused_computation.170 | convolution fusion | flops 1078984704 | bytes 11534336 | tf_op jit(solution)/shard_map/dot_general | solution.py:302
  159.4 3.3 fusion.109
  162.7 3.6 fusion.110
  166.3 6.0 %multiply_multiply_fusion.8 = (f32[512,1024]{1,0:T(8,128)}, f32[512,1024]{1,0:T(8,128)}) fusion(f32[512,1024]{1,0:T(8,128)S(1)} %fusion.109, f32[512,1024]{1,0:T(8,128)S(1)} %fusion.110, bf16[3,1024,1024]{1,2,0:T(8,128)(2,1)} %copy-done.14, bf16[256,1024]{1,0:T(8,128)(2,1)} %collective-permute-done.14, bf16[256,1024]{1,0:T(8,128)(2,1)} %collective-permute-done.13), kind=kOutput, calls=%fused_computation.169 | convolution fusion | flops 1078984704 | bytes 11534336 | tf_op jit(solution)/shard_map/dot_general | solution.py:302
  179.3 3.6 fusion.108
  182.9 5.9 %multiply_multiply_fusion.7 = (f32[512,1024]{1,0:T(8,128)}, f32[512,1024]{1,0:T(8,128)}) fusion(f32[512,1024]{1,0:T(8,128)S(1)} %fusion.107, f32[512,1024]{1,0:T(8,128)S(1)} %fusion.108, bf16[3,1024,1024]{1,2,0:T(8,128)(2,1)} %copy-done.14, bf16[256,1024]{1,0:T(8,128)(2,1)S(1)} %copy-done.68, bf16[256,1024]{1,0:T(8,128)(2,1)} %collective-permute-done.17), kind=kOutput, calls=%fused_computation.168 | convolution fusion | flops 1078984704 | bytes 11534336 | tf_op jit(solution)/shard_map/dot_general | solution.py:302
  223.0 4.6 fusion.40
  238.6 7.0 %fusion.43 = f32[1,1024,1024]{2,1,0:T(8,128)S(1)} fusion(bf16[2048,1024]{1,0:T(8,128)(2,1)} %copy-done.92, bf16[512,1024]{1,0:T(8,128)(2,1)S(1)} %get-tuple-element.97, bf16[512,1024]{1,0:T(8,128)(2,1)S(1)} %get-tuple-element.100, bf16[512,1024]{1,0:T(8,128)(2,1)S(1)} %copy-done.55, bf16[512,1024]{1,0:T(8,128)(2,1)S(1)} %get-tuple-element.94), kind=kOutput, calls=%fused_computation.59 | convolution fusion | flops 4311744512 | bytes 12582912 | tf_op jit(solution)/shard_map/dot_general | solution.py:384
  247.2 6.9 %fusion.46 = f32[1,1024,1024]{2,1,0:T(8,128)S(1)} fusion(bf16[2048,1024]{1,0:T(8,128)(2,1)} %copy-done.92, bf16[512,1024]{1,0:T(8,128)(2,1)S(1)} %get-tuple-element.96, bf16[512,1024]{1,0:T(8,128)(2,1)S(1)} %copy-done.56, bf16[512,1024]{1,0:T(8,128)(2,1)S(1)} %copy-done.53, bf16[512,1024]{1,0:T(8,128)(2,1)S(1)} %copy-done.51), kind=kOutput, calls=%fused_computation.60 | convolution fusion | flops 4311744512 | bytes 12582912 | tf_op jit(solution)/shard_map/dot_general | solution.py:384
  259.3 4.3 collective-permute-start.12
  263.8 12.0 %collective-permute-done.12 = bf16[272,1024]{1,0:T(8,128)(2,1)S(1)} collective-permute-done((bf16[272,1024]{1,0:T(8,128)(2,1)S(1)}, bf16[272,1024]{1,0:T(8,128)(2,1)S(1)}, u32[]{:S(2)}, u32[]{:S(2)}) %collective-permute-start.12) | collective-permute-done | bytes 557088 | tf_op jit(solution)/shard_map/ppermute | solution.py:141
  276.0 4.3 collective-permute-start.16
  280.6 11.1 %collective-permute-done.16 = bf16[272,1024]{1,0:T(8,128)(2,1)S(1)} collective-permute-done((bf16[272,1024]{1,0:T(8,128)(2,1)S(1)}, bf16[272,1024]{1,0:T(8,128)(2,1)S(1)}, u32[]{:S(2)}, u32[]{:S(2)}) %collective-permute-start.16) | collective-permute-done | bytes 557088 | tf_op jit(solution)/shard_map/ppermute | solution.py:141
  291.9 4.3 collective-permute-start.20
  296.3 10.3 %collective-permute-done.20 = bf16[272,1024]{1,0:T(8,128)(2,1)S(1)} collective-permute-done((bf16[272,1024]{1,0:T(8,128)(2,1)S(1)}, bf16[272,1024]{1,0:T(8,128)(2,1)S(1)}, u32[]{:S(2)}, u32[]{:S(2)}) %collective-permute-start.20) | collective-permute-done | bytes 557088 | tf_op jit(solution)/shard_map/ppermute | solution.py:141
  308.9 4.6 copy-done.3
  319.4 4.3 collective-permute-start.23
  329.7 5.9 %collective-permute-done.23 = bf16[256,1024]{1,0:T(8,128)(2,1)} collective-permute-done((bf16[256,1024]{1,0:T(8,128)(2,1)}, bf16[256,1024]{1,0:T(8,128)(2,1)}, u32[]{:S(2)}, u32[]{:S(2)}) %collective-permute-start.23) | collective-permute-done | bytes 524320 | tf_op jit(solution)/shard_map/ppermute | solution.py:141
  337.8 4.3 collective-permute-start.25
  345.6 8.0 %collective-permute-done.25 = bf16[256,1024]{1,0:T(8,128)(2,1)} collective-permute-done((bf16[256,1024]{1,0:T(8,128)(2,1)}, bf16[256,1024]{1,0:T(8,128)(2,1)}, u32[]{:S(2)}, u32[]{:S(2)}) %collective-permute-start.25) | collective-permute-done | bytes 524320 | tf_op jit(solution)/shard_map/ppermute | solution.py:141
  354.8 4.4 collective-permute-start.27
  362.1 7.0 %collective-permute-done.27 = bf16[256,1024]{1,0:T(8,128)(2,1)S(1)} collective-permute-done((bf16[256,1024]{1,0:T(8,128)(2,1)S(1)}, bf16[256,1024]{1,0:T(8,128)(2,1)S(1)}, u32[]{:S(2)}, u32[]{:S(2)}) %collective-permute-start.27) | collective-permute-done | bytes 524320 | tf_op jit(solution)/shard_map/ppermute | solution.py:141
  370.3 5.0 slice_add_fusion
  377.4 3.5 subtract_add_fusion
  383.4 4.6 fusion.180
  388.1 16.1 %fusion.77 = f32[512,4,1,64]{0,3,1,2:T(8,128)} fusion(f32[4,512,512,2]{2,1,3,0:T(8,128)} %fusion.180, f32[4,2,512,512]{2,3,1,0:T(8,128)} %copy-done.4, f32[4,2,512]{2,1,0:T(2,128)S(1)} %bitcast.217, bf16[512,4,2,32]{0,3,2,1:T(8,128)(2,1)} %copy-done.79, bf16[512,4,2,32]{0,3,2,1:T(8,128)(2,1)S(1)} %copy-done.78), kind=kOutput, calls=%fused_computation.126 | convolution fusion | flops 284168704 | bytes 17842176 | tf_op jit(solution)/shard_map/kgqs,qkgd->skd/dot_general | solution.py:408
  404.2 16.2 %fusion.75 = f32[512,4,2,64]{0,3,2,1:T(8,128)} fusion(f32[4,512,512,2]{2,1,3,0:T(8,128)} %fusion.180, f32[4,2,512,512]{2,3,1,0:T(8,128)} %copy-done.4, f32[4,2,512]{2,1,0:T(2,128)S(1)} %bitcast.218, bf16[512,4,32]{0,2,1:T(8,128)(2,1)} %copy-done.82, bf16[512,4,32]{0,2,1:T(8,128)(2,1)S(1)} %copy-done.81), kind=kOutput, calls=%fused_computation.123 | convolution fusion | flops 283644416 | bytes 18104320 | tf_op jit(solution)/shard_map/kgqs,skd->qkgd/dot_general | solution.py:407
  424.3 4.9 fusion.81
  435.3 6.9 %collective-permute-done.44 = bf16[128,1024]{1,0:T(8,128)(2,1)S(1)} collective-permute-done((bf16[128,1024]{1,0:T(8,128)(2,1)S(1)}, bf16[128,1024]{1,0:T(8,128)(2,1)S(1)}, u32[]{:S(2)}, u32[]{:S(2)}) %collective-permute-start.44) | collective-permute-done | bytes 262176 | tf_op jit(solution)/shard_map/ppermute | solution.py:135
  442.4 6.6 %collective-permute-done.33 = bf16[512,1024]{1,0:T(8,128)(2,1)S(1)} collective-permute-done((bf16[512,1024]{1,0:T(8,128)(2,1)S(1)}, bf16[512,1024]{1,0:T(8,128)(2,1)S(1)}, u32[]{:S(2)}, u32[]{:S(2)}) %collective-permute-start.33) | collective-permute-done | bytes 1048608 | tf_op jit(solution)/shard_map/ppermute | solution.py:135
  450.1 4.3 collective-permute-start.45
  456.4 4.0 collective-permute-done.47
  491.3 4.1 collective-permute-done.39
  499.6 39.7 %all-reduce = (f32[1024]{0:T(1024)}, f32[1024]{0:T(1024)}) all-reduce(f32[1024]{0:T(1024)S(1)} %get-tuple-element.58, f32[1024]{0:T(1024)S(1)} %copy-done.100), channel_id=1, replica_groups=mesh['ex'=16,'tp'=2] {'ex'}, use_global_device_ids=true, to_apply=%region_24.25 | all-reduce | flops 2048 | bytes 16384 | tf_op jit(solution)/shard_map/psum | solution.py:428
  551.5 9.4 %collective-permute-done.42 = bf16[512,1024]{1,0:T(8,128)(2,1)S(1)} collective-permute-done((bf16[512,1024]{1,0:T(8,128)(2,1)S(1)}, bf16[512,1024]{1,0:T(8,128)(2,1)S(1)}, u32[]{:S(2)}, u32[]{:S(2)}) %collective-permute-start.42) | collective-permute-done | bytes 1048608 | tf_op jit(solution)/shard_map/ppermute | solution.py:135
  (504 shorter events, 214.3 us)
Async XLA Ops:
  7.2 557.8 %all-reduce.3.cloned.1.call-start = ((), (), s32[]{:S(2)}) async-start(), calls=%async_computation | async-start | bytes 131072 | tf_op jit(solution)/shard_map/psum | solution.py:430
  9.6 23.2 %collective-permute-start.9 = (bf16[256,1024]{1,0:T(8,128)(2,1)}, bf16[256,1024]{1,0:T(8,128)(2,1)}, u32[]{:S(2)}, u32[]{:S(2)}) collective-permute-start(bf16[256,1024]{1,0:T(8,128)(2,1)} %get-tuple-element.77), channel_id=1, source_target_pairs={{0,24},{2,26},{4,28},{6,30},{8,0},{10,2},{12,4},{14,6},{16,8},{18,... | collective-permute-start | bytes 1572872 | tf_op jit(solution)/shard_map/ppermute | solution.py:141
  27.5 39.0 %collective-permute-start = (f32[512,1024]{1,0:T(8,128)}, f32[512,1024]{1,0:T(8,128)}, u32[]{:S(2)}, u32[]{:S(2)}) collective-permute-start(f32[512,1024]{1,0:T(8,128)} %fusion.179), channel_id=1, source_target_pairs={{0,1},{1,0},{2,3},{3,2},{4,5},{5,4},{6,7},{7,6},{8,9},{9,8},{10,11... | collective-permute-start | bytes 6291464 | tf_op jit(solution)/shard_map/ppermute | solution.py:71
  31.3 33.4 %collective-permute-start.1 = (bf16[3,1024,256]{1,2,0:T(8,128)(2,1)}, bf16[3,1024,256]{1,2,0:T(8,128)(2,1)}, u32[]{:S(2)}, u32[]{:S(2)}) collective-permute-start(bf16[3,1024,256]{1,2,0:T(8,128)(2,1)} %pad_maximum_fusion.3), channel_id=1, source_target_pairs={{0,2},{1,5},{2,0},{3,7},{4,6},{5,1},{6,4},{7,3},{8,10},{9,13},{10,... | collective-permute-start | bytes 4718600 | tf_op jit(solution)/shard_map/ppermute | solution.py:135
  32.8 14.4 %collective-permute-start.13 = (bf16[256,1024]{1,0:T(8,128)(2,1)}, bf16[256,1024]{1,0:T(8,128)(2,1)}, u32[]{:S(2)}, u32[]{:S(2)}) collective-permute-start(bf16[256,1024]{1,0:T(8,128)(2,1)} %collective-permute-done.9), channel_id=1, source_target_pairs={{0,24},{2,26},{4,28},{6,30},{8,0},{10,2},{12,4},{14,6},{16,8},{18,... | collective-permute-start | bytes 1572872 | tf_op jit(solution)/shard_map/ppermute | solution.py:141
  33.3 20.3 %collective-permute-start.10 = (bf16[256,1024]{1,0:T(8,128)(2,1)}, bf16[256,1024]{1,0:T(8,128)(2,1)}, u32[]{:S(2)}, u32[]{:S(2)}) collective-permute-start(bf16[256,1024]{1,0:T(8,128)(2,1)} %collective-permute-done.9), channel_id=1, source_target_pairs={{0,1},{1,0},{2,3},{3,2},{4,5},{5,4},{6,7},{7,6},{8,9},{9,8},{10,11... | collective-permute-start | bytes 1572872 | tf_op jit(solution)/shard_map/ppermute | solution.py:71
  47.2 13.8 %collective-permute-start.17 = (bf16[256,1024]{1,0:T(8,128)(2,1)}, bf16[256,1024]{1,0:T(8,128)(2,1)}, u32[]{:S(2)}, u32[]{:S(2)}) collective-permute-start(bf16[256,1024]{1,0:T(8,128)(2,1)} %collective-permute-done.13), channel_id=1, source_target_pairs={{0,24},{2,26},{4,28},{6,30},{8,0},{10,2},{12,4},{14,6},{16,8},{18,... | collective-permute-start | bytes 1572872 | tf_op jit(solution)/shard_map/ppermute | solution.py:141
  49.7 11.3 %collective-permute-start.14 = (bf16[256,1024]{1,0:T(8,128)(2,1)}, bf16[256,1024]{1,0:T(8,128)(2,1)}, u32[]{:S(2)}, u32[]{:S(2)}) collective-permute-start(bf16[256,1024]{1,0:T(8,128)(2,1)} %collective-permute-done.13), channel_id=1, source_target_pairs={{0,1},{1,0},{2,3},{3,2},{4,5},{5,4},{6,7},{7,6},{8,9},{9,8},{10,11... | collective-permute-start | bytes 1572872 | tf_op jit(solution)/shard_map/ppermute | solution.py:71
  61.0 15.9 %collective-permute-start.18 = (bf16[256,1024]{1,0:T(8,128)(2,1)}, bf16[256,1024]{1,0:T(8,128)(2,1)S(1)}, u32[]{:S(2)}, u32[]{:S(2)}) collective-permute-start(bf16[256,1024]{1,0:T(8,128)(2,1)} %collective-permute-done.17), channel_id=1, source_target_pairs={{0,1},{1,0},{2,3},{3,2},{4,5},{5,4},{6,7},{7,6},{8,9},{9,8},{10,11... | collective-permute-start | bytes 1572872 | tf_op jit(solution)/shard_map/ppermute | solution.py:71
  66.4 61.7 %collective-permute-start.2 = (bf16[3,1024,512]{1,2,0:T(8,128)(2,1)S(1)}, bf16[3,1024,512]{1,2,0:T(8,128)(2,1)S(1)}, u32[]{:S(2)}, u32[]{:S(2)}) collective-permute-start(bf16[3,1024,512]{1,2,0:T(8,128)(2,1)S(1)} %pad_maximum_fusion.2), channel_id=1, source_target_pairs={{0,4},{1,3},{2,6},{3,1},{4,0},{5,7},{6,2},{7,5},{8,12},{9,11},{10,... | collective-permute-start | bytes 9437192 | tf_op jit(solution)/shard_map/ppermute | solution.py:135
  72.6 16.3 %collective-permute-start.3 = (bf16[272,1024]{1,0:T(8,128)(2,1)S(1)}, bf16[272,1024]{1,0:T(8,128)(2,1)S(1)}, u32[]{:S(2)}, u32[]{:S(2)}) collective-permute-start(bf16[272,1024]{1,0:T(8,128)(2,1)S(1)} %maximum_maximum_fusion), channel_id=1, source_target_pairs={{0,24},{2,26},{4,28},{6,30},{8,0},{10,2},{12,4},{14,6},{16,8},{18,... | collective-permute-start | bytes 1671176 | tf_op jit(solution)/shard_map/ppermute | solution.py:141
  90.1 16.1 %collective-permute-start.5 = (bf16[272,1024]{1,0:T(8,128)(2,1)S(1)}, bf16[272,1024]{1,0:T(8,128)(2,1)S(1)}, u32[]{:S(2)}, u32[]{:S(2)}) collective-permute-start(bf16[272,1024]{1,0:T(8,128)(2,1)S(1)} %collective-permute-done.3), channel_id=1, source_target_pairs={{0,24},{2,26},{4,28},{6,30},{8,0},{10,2},{12,4},{14,6},{16,8},{18,... | collective-permute-start | bytes 1671176 | tf_op jit(solution)/shard_map/ppermute | solution.py:141
  106.4 16.9 %collective-permute-start.7 = (bf16[272,1024]{1,0:T(8,128)(2,1)S(1)}, bf16[272,1024]{1,0:T(8,128)(2,1)S(1)}, u32[]{:S(2)}, u32[]{:S(2)}) collective-permute-start(bf16[272,1024]{1,0:T(8,128)(2,1)S(1)} %collective-permute-done.5), channel_id=1, source_target_pairs={{0,24},{2,26},{4,28},{6,30},{8,0},{10,2},{12,4},{14,6},{16,8},{18,... | collective-permute-start | bytes 1671176 | tf_op jit(solution)/shard_map/ppermute | solution.py:141
  232.8 26.4 %collective-permute-start.11 = (bf16[256,1024]{1,0:T(8,128)(2,1)S(1)}, bf16[256,1024]{1,0:T(8,128)(2,1)S(1)}, u32[]{:S(2)}, u32[]{:S(2)}) collective-permute-start(bf16[256,1024]{1,0:T(8,128)(2,1)S(1)} %slice.306), channel_id=1, source_target_pairs={{0,1},{1,0},{2,3},{3,2},{4,5},{5,4},{6,7},{7,6},{8,9},{9,8},{10,11... | collective-permute-start | bytes 1572872 | tf_op jit(solution)/shard_map/ppermute | solution.py:71
  259.3 16.5 %collective-permute-start.12 = (bf16[272,1024]{1,0:T(8,128)(2,1)S(1)}, bf16[272,1024]{1,0:T(8,128)(2,1)S(1)}, u32[]{:S(2)}, u32[]{:S(2)}) collective-permute-start(bf16[272,1024]{1,0:T(8,128)(2,1)S(1)} %maximum_maximum_fusion.1), channel_id=1, source_target_pairs={{0,24},{2,26},{4,28},{6,30},{8,0},{10,2},{12,4},{14,6},{16,8},{18,... | collective-permute-start | bytes 1671176 | tf_op jit(solution)/shard_map/ppermute | solution.py:141
  263.7 16.8 %collective-permute-start.19 = (bf16[256,1024]{1,0:T(8,128)(2,1)S(1)}, bf16[256,1024]{1,0:T(8,128)(2,1)S(1)}, u32[]{:S(2)}, u32[]{:S(2)}) collective-permute-start(bf16[256,1024]{1,0:T(8,128)(2,1)S(1)} %slice.314), channel_id=1, source_target_pairs={{0,1},{1,0},{2,3},{3,2},{4,5},{5,4},{6,7},{7,6},{8,9},{9,8},{10,11... | collective-permute-start | bytes 1572872 | tf_op jit(solution)/shard_map/ppermute | solution.py:71
  276.0 15.7 %collective-permute-start.16 = (bf16[272,1024]{1,0:T(8,128)(2,1)S(1)}, bf16[272,1024]{1,0:T(8,128)(2,1)S(1)}, u32[]{:S(2)}, u32[]{:S(2)}) collective-permute-start(bf16[272,1024]{1,0:T(8,128)(2,1)S(1)} %maximum_add_fusion), channel_id=1, source_target_pairs={{0,24},{2,26},{4,28},{6,30},{8,0},{10,2},{12,4},{14,6},{16,8},{18,... | collective-permute-start | bytes 1671176 | tf_op jit(solution)/shard_map/ppermute | solution.py:141
  280.4 15.9 %collective-permute-start.21 = (bf16[256,1024]{1,0:T(8,128)(2,1)S(1)}, bf16[256,1024]{1,0:T(8,128)(2,1)S(1)}, u32[]{:S(2)}, u32[]{:S(2)}) collective-permute-start(bf16[256,1024]{1,0:T(8,128)(2,1)S(1)} %slice.318), channel_id=1, source_target_pairs={{0,1},{1,0},{2,3},{3,2},{4,5},{5,4},{6,7},{7,6},{8,9},{9,8},{10,11... | collective-permute-start | bytes 1572872 | tf_op jit(solution)/shard_map/ppermute | solution.py:71
  291.9 14.8 %collective-permute-start.20 = (bf16[272,1024]{1,0:T(8,128)(2,1)S(1)}, bf16[272,1024]{1,0:T(8,128)(2,1)S(1)}, u32[]{:S(2)}, u32[]{:S(2)}) collective-permute-start(bf16[272,1024]{1,0:T(8,128)(2,1)S(1)} %maximum_add_fusion.1), channel_id=1, source_target_pairs={{0,24},{2,26},{4,28},{6,30},{8,0},{10,2},{12,4},{14,6},{16,8},{18,... | collective-permute-start | bytes 1671176 | tf_op jit(solution)/shard_map/ppermute | solution.py:141
  306.9 11.6 %collective-permute-start.22 = (bf16[256,1024]{1,0:T(8,128)(2,1)S(1)}, bf16[256,1024]{1,0:T(8,128)(2,1)S(1)}, u32[]{:S(2)}, u32[]{:S(2)}) collective-permute-start(bf16[256,1024]{1,0:T(8,128)(2,1)S(1)} %slice.253), channel_id=1, source_target_pairs={{0,1},{1,0},{2,3},{3,2},{4,5},{5,4},{6,7},{7,6},{8,9},{9,8},{10,11... | collective-permute-start | bytes 1572872 | tf_op jit(solution)/shard_map/ppermute | solution.py:71
  315.6 54.7 %collective-permute-start.53 = (bf16[3,1024,512]{2,1,0:T(8,128)(2,1)}, bf16[3,1024,512]{2,1,0:T(8,128)(2,1)}, u32[]{:S(2)}, u32[]{:S(2)}) collective-permute-start(bf16[3,1024,512]{2,1,0:T(8,128)(2,1)} %slice.418), channel_id=1, source_target_pairs={{0,4},{1,3},{2,6},{3,1},{4,0},{5,7},{6,2},{7,5},{8,12},{9,11},{10,... | collective-permute-start | bytes 9437192 | tf_op jit(solution)/shard_map/ppermute | solution.py:135
  318.3 10.9 %collective-permute-start.24 = (bf16[256,1024]{1,0:T(8,128)(2,1)}, bf16[256,1024]{1,0:T(8,128)(2,1)}, u32[]{:S(2)}, u32[]{:S(2)}) collective-permute-start(bf16[256,1024]{1,0:T(8,128)(2,1)} %slice.255), channel_id=1, source_target_pairs={{0,1},{1,0},{2,3},{3,2},{4,5},{5,4},{6,7},{7,6},{8,9},{9,8},{10,11... | collective-permute-start | bytes 1572872 | tf_op jit(solution)/shard_map/ppermute | solution.py:71
  319.4 16.2 %collective-permute-start.23 = (bf16[256,1024]{1,0:T(8,128)(2,1)}, bf16[256,1024]{1,0:T(8,128)(2,1)}, u32[]{:S(2)}, u32[]{:S(2)}) collective-permute-start(bf16[256,1024]{1,0:T(8,128)(2,1)} %slice_add_fusion.6), channel_id=1, source_target_pairs={{0,24},{2,26},{4,28},{6,30},{8,0},{10,2},{12,4},{14,6},{16,8},{18,... | collective-permute-start | bytes 1572872 | tf_op jit(solution)/shard_map/ppermute | solution.py:141
  328.6 15.6 %collective-permute-start.30 = (bf16[256,1024]{1,0:T(8,128)(2,1)}, bf16[256,1024]{1,0:T(8,128)(2,1)}, u32[]{:S(2)}, u32[]{:S(2)}) collective-permute-start(bf16[256,1024]{1,0:T(8,128)(2,1)} %slice.321), channel_id=1, source_target_pairs={{0,1},{1,0},{2,3},{3,2},{4,5},{5,4},{6,7},{7,6},{8,9},{9,8},{10,11... | collective-permute-start | bytes 1572872 | tf_op jit(solution)/shard_map/ppermute | solution.py:71
  329.1 33.0 %collective-permute-start.28 = (bf16[256,1024]{1,0:T(8,128)(2,1)}, bf16[256,1024]{1,0:T(8,128)(2,1)}, u32[]{:S(2)}, u32[]{:S(2)}) collective-permute-start(bf16[256,1024]{1,0:T(8,128)(2,1)} %slice.259), channel_id=1, source_target_pairs={{0,1},{1,0},{2,3},{3,2},{4,5},{5,4},{6,7},{7,6},{8,9},{9,8},{10,11... | collective-permute-start | bytes 1572872 | tf_op jit(solution)/shard_map/ppermute | solution.py:71
  329.2 16.4 %collective-permute-start.26 = (bf16[256,1024]{1,0:T(8,128)(2,1)}, bf16[256,1024]{1,0:T(8,128)(2,1)}, u32[]{:S(2)}, u32[]{:S(2)}) collective-permute-start(bf16[256,1024]{1,0:T(8,128)(2,1)} %slice.257), channel_id=1, source_target_pairs={{0,1},{1,0},{2,3},{3,2},{4,5},{5,4},{6,7},{7,6},{8,9},{9,8},{10,11... | collective-permute-start | bytes 1572872 | tf_op jit(solution)/shard_map/ppermute | solution.py:71
  337.8 15.7 %collective-permute-start.25 = (bf16[256,1024]{1,0:T(8,128)(2,1)}, bf16[256,1024]{1,0:T(8,128)(2,1)}, u32[]{:S(2)}, u32[]{:S(2)}) collective-permute-start(bf16[256,1024]{1,0:T(8,128)(2,1)} %add_add_fusion.2), channel_id=1, source_target_pairs={{0,24},{2,26},{4,28},{6,30},{8,0},{10,2},{12,4},{14,6},{16,8},{18,... | collective-permute-start | bytes 1572872 | tf_op jit(solution)/shard_map/ppermute | solution.py:141
  354.8 14.3 %collective-permute-start.27 = (bf16[256,1024]{1,0:T(8,128)(2,1)S(1)}, bf16[256,1024]{1,0:T(8,128)(2,1)S(1)}, u32[]{:S(2)}, u32[]{:S(2)}) collective-permute-start(bf16[256,1024]{1,0:T(8,128)(2,1)S(1)} %add_add_fusion.1), channel_id=1, source_target_pairs={{0,24},{2,26},{4,28},{6,30},{8,0},{10,2},{12,4},{14,6},{16,8},{18,... | collective-permute-start | bytes 1572872 | tf_op jit(solution)/shard_map/ppermute | solution.py:141
  370.2 6.7 %collective-permute-start.29 = (bf16[256,1024]{1,0:T(8,128)(2,1)S(1)}, bf16[256,1024]{1,0:T(8,128)(2,1)S(1)}, u32[]{:S(2)}, u32[]{:S(2)}) collective-permute-start(bf16[256,1024]{1,0:T(8,128)(2,1)S(1)} %add_add_fusion), channel_id=1, source_target_pairs={{0,1},{1,0},{2,3},{3,2},{4,5},{5,4},{6,7},{7,6},{8,9},{9,8},{10,11... | collective-permute-start | bytes 1572872 | tf_op jit(solution)/shard_map/ppermute | solution.py:71
  376.8 56.5 %collective-permute-start.54 = (bf16[3,1024,256]{2,1,0:T(8,128)(2,1)}, bf16[3,1024,256]{2,1,0:T(8,128)(2,1)}, u32[]{:S(2)}, u32[]{:S(2)}) collective-permute-start(bf16[3,1024,256]{2,1,0:T(8,128)(2,1)} %slice.419), channel_id=1, source_target_pairs={{0,2},{1,5},{2,0},{3,7},{4,6},{5,1},{6,4},{7,3},{8,10},{9,13},{10,... | collective-permute-start | bytes 4718600 | tf_op jit(solution)/shard_map/ppermute | solution.py:135
  420.5 10.9 %collective-permute-start.43 = (bf16[256,1024]{1,0:T(8,128)(2,1)S(1)}, bf16[256,1024]{1,0:T(8,128)(2,1)S(1)}, u32[]{:S(2)}, u32[]{:S(2)}) collective-permute-start(bf16[256,1024]{1,0:T(8,128)(2,1)S(1)} %dynamic-slice_convert_fusion.1), channel_id=1, source_target_pairs={{0,4},{1,3},{2,6},{3,1},{4,0},{5,7},{6,2},{7,5},{8,12},{9,11},{10,... | collective-permute-start | bytes 1572872 | tf_op jit(solution)/shard_map/ppermute | solution.py:135
  431.2 17.8 %collective-permute-start.33 = (bf16[512,1024]{1,0:T(8,128)(2,1)S(1)}, bf16[512,1024]{1,0:T(8,128)(2,1)S(1)}, u32[]{:S(2)}, u32[]{:S(2)}) collective-permute-start(bf16[512,1024]{1,0:T(8,128)(2,1)S(1)} %dynamic-slice_convert_fusion), channel_id=1, source_target_pairs={{0,4},{1,3},{2,6},{3,1},{4,0},{5,7},{6,2},{7,5},{8,12},{9,11},{10,... | collective-permute-start | bytes 3145736 | tf_op jit(solution)/shard_map/ppermute | solution.py:135
  432.9 9.3 %collective-permute-start.44 = (bf16[128,1024]{1,0:T(8,128)(2,1)S(1)}, bf16[128,1024]{1,0:T(8,128)(2,1)S(1)}, u32[]{:S(2)}, u32[]{:S(2)}) collective-permute-start(bf16[128,1024]{1,0:T(8,128)(2,1)S(1)} %dynamic-slice_convert_fusion.3), channel_id=1, source_target_pairs={{0,2},{1,5},{2,0},{3,7},{4,6},{5,1},{6,4},{7,3},{8,10},{9,13},{10,... | collective-permute-start | bytes 786440 | tf_op jit(solution)/shard_map/ppermute | solution.py:135
  449.5 14.5 %collective-permute-start.34 = (bf16[256,1024]{1,0:T(8,128)(2,1)S(1)}, bf16[256,1024]{1,0:T(8,128)(2,1)S(1)}, u32[]{:S(2)}, u32[]{:S(2)}) collective-permute-start(bf16[256,1024]{1,0:T(8,128)(2,1)S(1)} %dynamic-slice_convert_fusion.2), channel_id=1, source_target_pairs={{0,2},{1,5},{2,0},{3,7},{4,6},{5,1},{6,4},{7,3},{8,10},{9,13},{10,... | collective-permute-start | bytes 1572872 | tf_op jit(solution)/shard_map/ppermute | solution.py:135
  456.3 41.2 %collective-permute-start.32 = (bf16[512,1024]{1,0:T(8,128)(2,1)S(1)}, bf16[512,1024]{1,0:T(8,128)(2,1)}, u32[]{:S(2)}, u32[]{:S(2)}) collective-permute-start(bf16[512,1024]{1,0:T(8,128)(2,1)S(1)} %fusion.72), channel_id=1, source_target_pairs={{0,1},{1,0},{2,3},{3,2},{4,5},{5,4},{6,7},{7,6},{8,9},{9,8},{10,11... | collective-permute-start | bytes 3145736 | tf_op jit(solution)/shard_map/ppermute | solution.py:71
  461.1 11.9 %collective-permute-start.48 = (bf16[32,1024]{1,0:T(8,128)(2,1)}, bf16[32,1024]{1,0:T(8,128)(2,1)}, u32[]{:S(2)}, u32[]{:S(2)}) collective-permute-start(bf16[32,1024]{1,0:T(8,128)(2,1)} %get-tuple-element.79), channel_id=1, source_target_pairs={{0,24},{2,26},{4,28},{6,30},{8,0},{10,2},{12,4},{14,6},{16,8},{18,... | collective-permute-start | bytes 196616 | tf_op jit(solution)/shard_map/ppermute | solution.py:141
  466.7 10.1 %collective-permute-start.35 = (bf16[64,1024]{1,0:T(8,128)(2,1)}, bf16[64,1024]{1,0:T(8,128)(2,1)S(1)}, u32[]{:S(2)}, u32[]{:S(2)}) collective-permute-start(bf16[64,1024]{1,0:T(8,128)(2,1)} %get-tuple-element.138), channel_id=1, source_target_pairs={{0,24},{2,26},{4,28},{6,30},{8,0},{10,2},{12,4},{14,6},{16,8},{18,... | collective-permute-start | bytes 393224 | tf_op jit(solution)/shard_map/ppermute | solution.py:141
  466.7 11.8 %collective-permute-start.37 = (bf16[64,1024]{1,0:T(8,128)(2,1)}, bf16[64,1024]{1,0:T(8,128)(2,1)}, u32[]{:S(2)}, u32[]{:S(2)}) collective-permute-start(bf16[64,1024]{1,0:T(8,128)(2,1)} %get-tuple-element.139), channel_id=1, source_target_pairs={{0,8},{2,10},{4,12},{6,14},{8,16},{10,18},{12,20},{14,22},{16,24},... | collective-permute-start | bytes 393224 | tf_op jit(solution)/shard_map/ppermute | solution.py:141
  468.8 12.9 %collective-permute-start.36 = (bf16[64,1024]{1,0:T(8,128)(2,1)}, bf16[64,1024]{1,0:T(8,128)(2,1)}, u32[]{:S(2)}, u32[]{:S(2)}) collective-permute-start(bf16[64,1024]{1,0:T(8,128)(2,1)} %get-tuple-element.140), channel_id=1, source_target_pairs={{0,16},{2,18},{4,20},{6,22},{8,24},{10,26},{12,28},{14,30},{16,0},... | collective-permute-start | bytes 393224 | tf_op jit(solution)/shard_map/ppermute | solution.py:141
  473.1 12.8 %collective-permute-start.49 = (bf16[32,1024]{1,0:T(8,128)(2,1)}, bf16[32,1024]{1,0:T(8,128)(2,1)S(1)}, u32[]{:S(2)}, u32[]{:S(2)}) collective-permute-start(bf16[32,1024]{1,0:T(8,128)(2,1)} %get-tuple-element.79), channel_id=1, source_target_pairs={{0,16},{2,18},{4,20},{6,22},{8,24},{10,26},{12,28},{14,30},{16,0},... | collective-permute-start | bytes 196616 | tf_op jit(solution)/shard_map/ppermute | solution.py:141
  476.8 9.1 %collective-permute-start.50 = (bf16[32,1024]{1,0:T(8,128)(2,1)}, bf16[32,1024]{1,0:T(8,128)(2,1)S(1)}, u32[]{:S(2)}, u32[]{:S(2)}) collective-permute-start(bf16[32,1024]{1,0:T(8,128)(2,1)} %get-tuple-element.79), channel_id=1, source_target_pairs={{0,8},{2,10},{4,12},{6,14},{8,16},{10,18},{12,20},{14,22},{16,24},... | collective-permute-start | bytes 196616 | tf_op jit(solution)/shard_map/ppermute | solution.py:141
  483.5 7.1 %collective-permute-start.38 = (bf16[64,1024]{1,0:T(8,128)(2,1)S(1)}, bf16[64,1024]{1,0:T(8,128)(2,1)S(1)}, u32[]{:S(2)}, u32[]{:S(2)}) collective-permute-start(bf16[64,1024]{1,0:T(8,128)(2,1)S(1)} %get-tuple-element.83), channel_id=1, source_target_pairs={{0,24},{2,26},{4,28},{6,30},{8,0},{10,2},{12,4},{14,6},{16,8},{18,... | collective-permute-start | bytes 393224 | tf_op jit(solution)/shard_map/ppermute | solution.py:141
  485.9 9.5 %collective-permute-start.39 = (bf16[64,1024]{1,0:T(8,128)(2,1)S(1)}, bf16[64,1024]{1,0:T(8,128)(2,1)S(1)}, u32[]{:S(2)}, u32[]{:S(2)}) collective-permute-start(bf16[64,1024]{1,0:T(8,128)(2,1)S(1)} %get-tuple-element.83), channel_id=1, source_target_pairs={{0,16},{2,18},{4,20},{6,22},{8,24},{10,26},{12,28},{14,30},{16,0},... | collective-permute-start | bytes 393224 | tf_op jit(solution)/shard_map/ppermute | solution.py:141
  486.0 53.4 %collective-permute-start.51 = (bf16[128,1024]{1,0:T(8,128)(2,1)S(1)}, bf16[128,1024]{1,0:T(8,128)(2,1)}, u32[]{:S(2)}, u32[]{:S(2)}) collective-permute-start(bf16[128,1024]{1,0:T(8,128)(2,1)S(1)} %constant_dynamic-update-slice_fusion.16), channel_id=1, source_target_pairs={{0,2},{1,5},{2,0},{3,7},{4,6},{5,1},{6,4},{7,3},{8,10},{9,13},{10,... | collective-permute-start | bytes 786440 | tf_op jit(solution)/shard_map/ppermute | solution.py:135
  487.2 8.9 %collective-permute-start.40 = (bf16[64,1024]{1,0:T(8,128)(2,1)S(1)}, bf16[64,1024]{1,0:T(8,128)(2,1)S(1)}, u32[]{:S(2)}, u32[]{:S(2)}) collective-permute-start(bf16[64,1024]{1,0:T(8,128)(2,1)S(1)} %get-tuple-element.83), channel_id=1, source_target_pairs={{0,8},{2,10},{4,12},{6,14},{8,16},{10,18},{12,20},{14,22},{16,24},... | collective-permute-start | bytes 393224 | tf_op jit(solution)/shard_map/ppermute | solution.py:141
  496.7 43.8 %collective-permute-start.41 = (bf16[256,1024]{1,0:T(8,128)(2,1)}, bf16[256,1024]{1,0:T(8,128)(2,1)}, u32[]{:S(2)}, u32[]{:S(2)}) collective-permute-start(bf16[256,1024]{1,0:T(8,128)(2,1)} %constant_dynamic-update-slice_fusion.20), channel_id=1, source_target_pairs={{0,2},{1,5},{2,0},{3,7},{4,6},{5,1},{6,4},{7,3},{8,10},{9,13},{10,... | collective-permute-start | bytes 1572872 | tf_op jit(solution)/shard_map/ppermute | solution.py:135
  540.5 9.2 %collective-permute-start.52 = (bf16[256,1024]{1,0:T(8,128)(2,1)S(1)}, bf16[256,1024]{1,0:T(8,128)(2,1)S(1)}, u32[]{:S(2)}, u32[]{:S(2)}) collective-permute-start(bf16[256,1024]{1,0:T(8,128)(2,1)S(1)} %pad_maximum_fusion.20), channel_id=1, source_target_pairs={{0,4},{1,3},{2,6},{3,1},{4,0},{5,7},{6,2},{7,5},{8,12},{9,11},{10,... | collective-permute-start | bytes 1572872 | tf_op jit(solution)/shard_map/ppermute | solution.py:135
  541.9 19.1 %collective-permute-start.42 = (bf16[512,1024]{1,0:T(8,128)(2,1)S(1)}, bf16[512,1024]{1,0:T(8,128)(2,1)S(1)}, u32[]{:S(2)}, u32[]{:S(2)}) collective-permute-start(bf16[512,1024]{1,0:T(8,128)(2,1)S(1)} %pad_maximum_fusion.9), channel_id=1, source_target_pairs={{0,4},{1,3},{2,6},{3,1},{4,0},{5,7},{6,2},{7,5},{8,12},{9,11},{10,... | collective-permute-start | bytes 3145736 | tf_op jit(solution)/shard_map/ppermute | solution.py:135
  (121 other events, 920.6 us)
Sparse Core Ops, SparseCore 0:
  344.3 100.0 all-reduce.2
